TPU v7x, 32 devices: a whole 2x2x4 slice. The times are simulated.
32 devices in a mesh: query: 4 (over x, core), item: 8 (over z, y).
Axes of the slice: x: 2, y: 2, z: 4, core: 2. Of those that a mesh axis runs over, the one named last changes fastest.
Arguments:
- queries: bfloat16 [12288, 1024], P(('query', 'item')), may hold values from -6 to 6
- item_table: bfloat16 [16384, 1024], P('item'), may hold values from -6 to 6
- w_query: bfloat16 [1024, 512], replicated, may hold values from -0.1875 to 0.1875
- w_item_in: bfloat16 [1024, 1024], replicated, may hold values from -0.1875 to 0.1875
- w_item_out: bfloat16 [1024, 512], replicated, may hold values from -0.1875 to 0.1875
- pos_owner: int32 [12288, 1], P(('query', 'item')), may hold values from 0 to 7; in each aligned block of 384 rows (0 to 383, 384 to 767, ...) at most 96 rows name the same one
- pos_rows: int32 [12288], P(('query', 'item')), may hold values from 0 to 2047
- neg_owner: int32 [4, 1024, 1], P('query'), may hold values from 0 to 7; in each aligned block of 1024 rows (0 to 1023, 1024 to 2047, ..., all dimensions but the last counted through in order) at most 256 rows name the same one
- neg_rows: int32 [4, 1024], P('query'), may hold values from 0 to 2047
- neg_logq: float32 [4, 1024], P('query'), may hold values from 7 to 8
Outputs:
- grad_query: float32 [1024, 512], P('item', 'query')
- grad_item_in: float32 [1024, 1024], P('item', 'query')
- grad_item_out: float32 [1024, 512], P('item', 'query')
Inputs may be any that keep to these rules, and one draw needn't show every extreme that they name: `pos_owner`: among the 384 rows of one device no owner is named more than 96 times, a bound that some block reaches. `neg_owner`: among the 1024 negatives of one group no owner is named more than 256 times, a bound that some block reaches.
All inputs are finite; a program needn't handle non-finite values.
Results may differ from a plain program's by a relative error of at most 0.0065.
Values may be sent and summed in bfloat16 or wider, within the bound.
A program may use at most 128 MiB of HBM per device.

v0:
```python
import math

import jax
import jax.numpy as jnp
from jax import lax
from jax.sharding import PartitionSpec as P

TAU = 0.02
EPS = 1e-06


def slot_numbers(owners, owner_count):
    onehot = (owners[:, None] == jnp.arange(owner_count, dtype=jnp.int32)[None, :]).astype(
        jnp.int32
    )
    before = jnp.cumsum(onehot, axis=0) - onehot
    return jnp.sum(before * onehot, axis=1)


def item_tower(features, w_item_in, w_item_out):
    hidden_pre = jnp.dot(features, w_item_in, preferred_element_type=jnp.float32)
    hidden = jax.nn.silu(hidden_pre).astype(jnp.bfloat16)
    output = jnp.dot(hidden, w_item_out, preferred_element_type=jnp.float32)
    inverse = lax.rsqrt(jnp.sum(output * output, axis=-1, keepdims=True) + EPS)
    unit = output * inverse
    return (hidden_pre, hidden, inverse, unit, unit.astype(jnp.bfloat16))


def tower_grads(features, hidden_pre, hidden, inverse, unit, upstream, w_item_out):
    out_grad = (
        inverse * (upstream - unit * jnp.sum(unit * upstream, axis=-1, keepdims=True))
    ).astype(jnp.bfloat16)
    hidden_grad = lax.dot_general(
        out_grad, w_item_out, (((1,), (1,)), ((), ())), preferred_element_type=jnp.float32
    )
    sigma = jax.nn.sigmoid(hidden_pre)
    pre_grad = (hidden_grad * (sigma * (1.0 + hidden_pre * (1.0 - sigma)))).astype(jnp.bfloat16)
    grad_out = lax.dot_general(
        hidden, out_grad, (((0,), (0,)), ((), ())), preferred_element_type=jnp.float32
    )
    grad_in = lax.dot_general(
        features, pre_grad, (((0,), (0,)), ((), ())), preferred_element_type=jnp.float32
    )
    return (grad_in, grad_out)


def on_device(
    queries,
    item_table,
    w_query,
    w_item_in,
    w_item_out,
    pos_owner,
    pos_rows,
    neg_owner,
    neg_rows,
    neg_logq,
):
    owner_count = lax.axis_size("item")
    query_count = queries.shape[0]
    total_queries = query_count * owner_count * lax.axis_size("query")
    loss_scale = 1.0 / math.sqrt(total_queries)
    my_index = lax.axis_index("item")
    width = w_item_out.shape[1]
    negatives = neg_rows.shape[1]
    capacity = 2 * (negatives // owner_count)
    pos_capacity = max(2, 2 * query_count // owner_count)
    neg_owners = neg_owner[0, :, 0]
    neg_slots = slot_numbers(neg_owners, owner_count)
    slot_rows = (
        jnp.zeros((owner_count, capacity), jnp.int32).at[neg_owners, neg_slots].set(neg_rows[0])
    )
    slot_logq = (
        jnp.zeros((owner_count, capacity), jnp.float32).at[neg_owners, neg_slots].set(neg_logq[0])
    )
    slot_live = jnp.zeros((owner_count, capacity), jnp.bool_).at[neg_owners, neg_slots].set(True)
    own_rows = lax.dynamic_index_in_dim(slot_rows, my_index, 0, keepdims=False)
    pos_owners = pos_owner[:, 0]
    pos_slots = slot_numbers(pos_owners, owner_count)
    request = (
        jnp.zeros((owner_count, pos_capacity), jnp.int32).at[pos_owners, pos_slots].set(pos_rows)
    )
    asked = lax.all_to_all(request, "item", split_axis=0, concat_axis=0, tiled=True)
    features = jnp.concatenate(
        [jnp.take(item_table, own_rows, axis=0), jnp.take(item_table, asked.reshape(-1), axis=0)],
        axis=0,
    )
    hidden_pre, hidden, inverse, unit, item_embed = item_tower(features, w_item_in, w_item_out)
    neg_embed_own = item_embed[:capacity]
    pos_embed_own = item_embed[capacity:].reshape(owner_count, pos_capacity, width)
    returned = lax.all_to_all(pos_embed_own, "item", split_axis=0, concat_axis=0, tiled=True)
    pos_embed = returned[pos_owners, pos_slots]
    neg_embed = lax.all_gather(neg_embed_own, "item", axis=0, tiled=True)
    query_pre = jnp.dot(queries, w_query, preferred_element_type=jnp.float32)
    query_scale = lax.rsqrt(jnp.sum(query_pre * query_pre, axis=-1, keepdims=True) + EPS)
    query_unit = query_pre * query_scale
    query_embed = query_unit.astype(jnp.bfloat16)
    scores = lax.dot_general(
        query_embed, neg_embed, (((1,), (1,)), ((), ())), preferred_element_type=jnp.float32
    )
    logits = scores / TAU - slot_logq.reshape(-1)[None, :]
    weights_exp = jnp.where(slot_live.reshape(-1)[None, :], jnp.exp(logits), 0.0)
    pos_logit = (
        jnp.sum(query_embed.astype(jnp.float32) * pos_embed.astype(jnp.float32), axis=-1) / TAU
    )
    pos_exp = jnp.exp(pos_logit)
    total = pos_exp + jnp.sum(weights_exp, axis=-1)
    neg_weight = (loss_scale * weights_exp / total[:, None]).astype(jnp.bfloat16)
    pos_weight = loss_scale * (pos_exp / total - 1.0)
    query_grad = (
        jnp.dot(neg_weight, neg_embed, preferred_element_type=jnp.float32)
        + pos_weight[:, None] * pos_embed.astype(jnp.float32)
    ) / TAU
    pre_grad_query = (
        query_scale
        * (query_grad - query_unit * jnp.sum(query_unit * query_grad, axis=-1, keepdims=True))
    ).astype(jnp.bfloat16)
    grad_query = lax.dot_general(
        queries, pre_grad_query, (((0,), (0,)), ((), ())), preferred_element_type=jnp.float32
    )
    pos_grad = pos_weight[:, None] * query_embed.astype(jnp.float32) / TAU
    pos_back = (
        jnp.zeros((owner_count, pos_capacity, width), jnp.float32)
        .at[pos_owners, pos_slots]
        .set(pos_grad)
    )
    pos_grad_own = lax.all_to_all(
        pos_back, "item", split_axis=0, concat_axis=0, tiled=True
    ).reshape(-1, width)
    neg_grad_own = lax.psum_scatter(
        lax.dot_general(
            neg_weight, query_embed, (((0,), (0,)), ((), ())), preferred_element_type=jnp.float32
        )
        / TAU,
        "item",
        scatter_dimension=0,
        tiled=True,
    )
    upstream = jnp.concatenate([neg_grad_own, pos_grad_own], axis=0)
    grad_in, grad_out = tower_grads(
        features, hidden_pre, hidden, inverse, unit, upstream, w_item_out
    )
    reduced = (
        lax.psum_scatter(grad_query, "item", scatter_dimension=0, tiled=True),
        lax.psum_scatter(grad_in, "item", scatter_dimension=0, tiled=True),
        lax.psum_scatter(grad_out, "item", scatter_dimension=0, tiled=True),
    )
    final = (
        lax.psum_scatter(reduced[0], "query", scatter_dimension=1, tiled=True),
        lax.psum_scatter(reduced[1], "query", scatter_dimension=1, tiled=True),
        lax.psum_scatter(reduced[2], "query", scatter_dimension=1, tiled=True),
    )
    return (final[0], final[1], final[2])


def solution(mesh):
    return jax.shard_map(
        on_device,
        mesh=mesh,
        in_specs=(
            P(("query", "item"), None),
            P("item", None),
            P(),
            P(),
            P(),
            P(("query", "item"), None),
            P(("query", "item")),
            P("query", None, None),
            P("query", None),
            P("query", None),
        ),
        out_specs=(P("item", "query"), P("item", "query"), P("item", "query")),
        check_vma=False,
    )
```

profile of v0, /device:TPU:0, one launch (start us, length us, event | category | flops | bytes accessed | tf_op | source)
XLA Modules:
  0.0 594.2 jit_solution(4026485691343549929)
XLA Ops:
  10.6 58.5 %scatter_fusion = s32[8,96]{1,0:T(8,128)} fusion(s32[8,96]{1,0:T(8,128)} %broadcast_in_dim.80, s32[384]{0:T(512)S(1)} %get-tuple-element.13, s32[384]{0:T(512)} %param.16), kind=kCustom, calls=%fused_computation.3 | custom fusion | bytes 7680 | tf_op jit(solution)/shard_map/scatter | solution.py:81
  69.0 7.3 %all-to-all-start = ((s32[8,1,96]{2,1,0:T(1,128)}), s32[8,1,96]{2,1,0:T(1,128)S(1)}, u32[]{:S(2)}, u32[]{:S(2)}) async-start(s32[8,1,96]{2,1,0:T(1,128)} %bitcast.12), calls=%async_computation | async-start | bytes 8192 | tf_op jit(solution)/shard_map/all_to_all | solution.py:83
  79.4 4.5 scatter_custom_fusion.3
  84.0 4.3 gather_fusion
  89.8 7.3 %gather_fusion.1 = bf16[768,1024]{1,0:T(8,128)(2,1)} fusion(bf16[2048,1024]{1,0:T(8,128)(2,1)} %param.11, s32[1024]{0:T(1024)S(1)} %pad_clamp_fusion), kind=kCustom, calls=%fused_computation.1 | custom fusion | bytes 3148800 | tf_op jit(solution)/shard_map/jit(_take)/gather | solution.py:85
  98.8 4.6 multiply_convert_fusion.1
  108.1 5.9 %all-to-all-start.1 = ((bf16[8,96,512]{2,1,0:T(8,128)(2,1)}), bf16[8,96,512]{2,1,0:T(8,128)(2,1)S(1)}, u32[]{:S(2)}, u32[]{:S(2)}) async-start(bf16[8,96,512]{2,1,0:T(8,128)(2,1)} %bitcast.69), calls=%async_computation.1 | async-start | bytes 1572864 | tf_op jit(solution)/shard_map/all_to_all | solution.py:91
  114.3 4.3 scatter_custom_fusion.2
  118.7 4.5 scatter_custom_fusion.4
  123.1 3.0 multiply_reduce_fusion.3
  126.1 16.1 %all-to-all-done.1 = bf16[8,96,512]{2,1,0:T(8,128)(2,1)S(1)} async-done(((bf16[8,96,512]{2,1,0:T(8,128)(2,1)}), bf16[8,96,512]{2,1,0:T(8,128)(2,1)S(1)}, u32[]{:S(2)}, u32[]{:S(2)}) %all-to-all-start.1) | async-done | bytes 786464 | tf_op jit(solution)/shard_map/all_to_all | solution.py:91
  142.2 3.9 gather_fusion.2
  147.5 19.1 %all-gather.2.cloned.1.call-done = bf16[2048,512]{1,0:T(8,128)(2,1)} async-done(((bf16[256,512]{1,0:T(8,128)(2,1)}), bf16[2048,512]{1,0:T(8,128)(2,1)}) %all-gather.2.cloned.1.call-update) | async-done | bytes 2097168 | tf_op jit(solution)/shard_map/all_gather | solution.py:93
  171.1 3.3 convolution_multiply_fusion
  175.6 3.8 multiply_reduce_fusion.2
  184.2 49.9 %scatter_fusion.1 = f32[8,96,512]{2,1,0:T(8,128)} fusion(f32[8,96,512]{2,1,0:T(8,128)} %broadcast_in_dim.85, s32[384]{0:T(512)S(1)} %get-tuple-element.13, f32[384,512]{1,0:T(8,128)S(1)} %fusion.3), kind=kCustom, calls=%fused_computation.4 | custom fusion | bytes 2362368 | tf_op jit(solution)/shard_map/scatter | solution.py:125
  234.1 57.0 %all_to_all.19 = f32[8,96,512]{2,1,0:T(8,128)} all-to-all(f32[8,96,512]{2,1,0:T(8,128)} %scatter_fusion.1), channel_id=1, replica_groups=mesh['query'=4,'item'=8] {'item'}, dimensions={0} | all-to-all | bytes 3145728 | tf_op jit(solution)/shard_map/all_to_all | solution.py:127
  298.8 9.3 %fusion = f32[1024,1024]{1,0:T(8,128)} fusion(f32[1024,1024]{1,0:T(8,128)} %get-tuple-element.21, bf16[1024,512]{1,0:T(8,128)(2,1)S(1)} %multiply_convert_fusion.2, bf16[1024,512]{1,0:T(8,128)(2,1)} %param.14, bf16[768,1024]{1,0:T(8,128)(2,1)} %copy-done.6, bf16[256,1024]{1,0:T(8,128)(2,1)} %copy-done.10), kind=kOutput, calls=%fused_computation.20 | convolution fusion | flops 3234856960 | bytes 12582912 | tf_op jit(solution)/shard_map/dot_general | solution.py:41
  308.1 47.6 %reduce-scatter.8.cloned.1.call-done = f32[128,512]{0,1:T(8,128)} async-done(((f32[1024,512]{0,1:T(8,128)}), f32[128,512]{0,1:T(8,128)}) %reduce-scatter.8.cloned.1.call-update) | async-done | bytes 262160 | tf_op jit(solution)/shard_map/reduce_scatter | solution.py:144
  355.8 70.4 %reduce-scatter.18.cloned.1.call-done = f32[128,512]{1,0:T(8,128)} async-done(((f32[1024,512]{1,0:T(8,128)}), f32[128,512]{1,0:T(8,128)}) %reduce-scatter.18.cloned.1.call-update) | async-done | bytes 262160 | tf_op jit(solution)/shard_map/reduce_scatter | solution.py:146
  426.3 90.9 %reduce-scatter.14.cloned.1.call-done = f32[128,1024]{1,0:T(8,128)} async-done(((f32[1024,1024]{1,0:T(8,128)}), f32[128,1024]{1,0:T(8,128)}) %reduce-scatter.14.cloned.1.call-update) | async-done | bytes 524304 | tf_op jit(solution)/shard_map/reduce_scatter | solution.py:145
  517.2 22.1 %reduce-scatter.10.cloned.1.call-done = f32[128,128]{0,1:T(8,128)} async-done(((f32[128,512]{0,1:T(8,128)}), f32[128,128]{0,1:T(8,128)}) %reduce-scatter.10.cloned.1.call-update) | async-done | bytes 65552 | tf_op jit(solution)/shard_map/reduce_scatter | solution.py:149
  540.9 21.7 %reduce-scatter.20.cloned.1.call-done = f32[128,128]{1,0:T(8,128)} async-done(((f32[128,512]{1,0:T(8,128)}), f32[128,128]{1,0:T(8,128)}) %reduce-scatter.20.cloned.1.call-update) | async-done | bytes 65552 | tf_op jit(solution)/shard_map/reduce_scatter | solution.py:151
  562.6 24.7 %reduce-scatter.16.cloned.1.call-done = f32[128,256]{1,0:T(8,128)} async-done(((f32[128,1024]{1,0:T(8,128)}), f32[128,256]{1,0:T(8,128)}) %reduce-scatter.16.cloned.1.call-update) | async-done | bytes 131088 | tf_op jit(solution)/shard_map/reduce_scatter | solution.py:150
  (102 shorter events, 35.7 us)
Async XLA Ops:
  7.2 91.6 %copy-start = (bf16[1024,1024]{1,0:T(8,128)(2,1)S(1)}, bf16[1024,1024]{1,0:T(8,128)(2,1)}, u32[]{:S(2)}) copy-start(bf16[1024,1024]{1,0:T(8,128)(2,1)} %param.13) | copy-start | bytes 6291460
  10.6 65.8 %copy-start.11 = (s32[1,1024,1]{1,2,0:T(1,128)S(1)}, s32[1,1024,1]{1,2,0:T(1,128)}, u32[]{:S(2)}) copy-start(s32[1,1024,1]{1,2,0:T(1,128)} %param.17) | copy-start | bytes 12292
  10.6 68.7 %copy-start.13 = (s32[2]{0:T(128)S(1)}, s32[2]{0:T(128)}, u32[]{:S(2)}) copy-start(s32[2]{0:T(128)} %constant.93) | copy-start | bytes 28
  10.6 68.8 %copy-start.12 = (s32[2]{0:T(128)S(1)}, s32[2]{0:T(128)}, u32[]{:S(2)}) copy-start(s32[2]{0:T(128)} %constant.90) | copy-start | bytes 28
  69.0 19.4 %all-to-all-start = ((s32[8,1,96]{2,1,0:T(1,128)}), s32[8,1,96]{2,1,0:T(1,128)S(1)}, u32[]{:S(2)}, u32[]{:S(2)}) async-start(s32[8,1,96]{2,1,0:T(1,128)} %bitcast.12), calls=%async_computation | async-start | bytes 8192 | tf_op jit(solution)/shard_map/all_to_all | solution.py:83
  76.3 90.3 %all-gather.2.cloned.1.call-start = ((), (), s32[]{:S(2)}) async-start(), calls=%async_computation.10 | async-start | bytes 2359296 | tf_op jit(solution)/shard_map/all_gather | solution.py:93
  88.4 10.4 %copy-start.10 = (bf16[256,1024]{1,0:T(8,128)(2,1)}, bf16[256,1024]{1,0:T(8,128)(2,1)S(1)}, u32[]{:S(2)}) copy-start(bf16[256,1024]{1,0:T(8,128)(2,1)S(1)} %broadcast_select_fusion.1) | copy-start | bytes 1572868
  98.8 4.7 copy-start.6
  98.8 4.7 copy-start.14
  108.1 34.1 %all-to-all-start.1 = ((bf16[8,96,512]{2,1,0:T(8,128)(2,1)}), bf16[8,96,512]{2,1,0:T(8,128)(2,1)S(1)}, u32[]{:S(2)}, u32[]{:S(2)}) async-start(bf16[8,96,512]{2,1,0:T(8,128)(2,1)} %bitcast.69), calls=%async_computation.1 | async-start | bytes 1572864 | tf_op jit(solution)/shard_map/all_to_all | solution.py:91
  114.1 177.0 %reduce-scatter.12.cloned.1.call-start = ((), (), s32[]{:S(2)}) async-start(), calls=%async_computation.13 | async-start | bytes 4718592 | tf_op jit(solution)/shard_map/reduce_scatter | solution.py:130
  147.5 22.0 %copy-start.7 = (bf16[384,512]{1,0:T(8,128)(2,1)}, bf16[384,512]{1,0:T(8,128)(2,1)S(1)}, u32[]{:S(2)}) copy-start(bf16[384,512]{1,0:T(8,128)(2,1)S(1)} %get-tuple-element.15) | copy-start | bytes 1179652
  169.4 1.7 copy-start.17
  174.5 181.2 %reduce-scatter.8.cloned.1.call-start = ((), (), s32[]{:S(2)}) async-start(), calls=%async_computation.11 | async-start | bytes 2359296 | tf_op jit(solution)/shard_map/reduce_scatter | solution.py:144
  175.6 3.8 copy-start.9
  181.7 244.6 %reduce-scatter.18.cloned.1.call-start = ((), (), s32[]{:S(2)}) async-start(), calls=%async_computation.16 | async-start | bytes 2359296 | tf_op jit(solution)/shard_map/reduce_scatter | solution.py:146
  291.0 2.9 copy-start.2
  291.0 3.3 copy-start.3
  291.0 3.4 copy-start.5
  294.4 1.6 copy-start.16
  298.7 218.5 %reduce-scatter.14.cloned.1.call-start = ((), (), s32[]{:S(2)}) async-start(), calls=%async_computation.14 | async-start | bytes 4718592 | tf_op jit(solution)/shard_map/reduce_scatter | solution.py:145
  308.1 231.3 %reduce-scatter.10.cloned.1.call-start = ((), (), s32[]{:S(2)}) async-start(), calls=%async_computation.12 | async-start | bytes 327680 | tf_op jit(solution)/shard_map/reduce_scatter | solution.py:149
  355.8 206.9 %reduce-scatter.20.cloned.1.call-start = ((), (), s32[]{:S(2)}) async-start(), calls=%async_computation.17 | async-start | bytes 327680 | tf_op jit(solution)/shard_map/reduce_scatter | solution.py:151
  426.3 161.1 %reduce-scatter.16.cloned.1.call-start = ((), (), s32[]{:S(2)}) async-start(), calls=%async_computation.15 | async-start | bytes 655360 | tf_op jit(solution)/shard_map/reduce_scatter | solution.py:150
  (4 other events, 4.9 us)
Sparse Core Ops, SparseCore 0:
  107.2 59.3 all-gather.1
  174.6 110.8 reduce-scatter.11
  289.5 66.1 reduce-scatter.7
  359.5 66.6 reduce-scatter.17
  430.2 87.0 reduce-scatter.13
  519.5 19.7 reduce-scatter.9
  542.5 20.0 reduce-scatter.19
  565.7 21.6 reduce-scatter.15
where the time goes:
time: 598 us; the launch traced here: 594 us
  waiting for transfers between devices  313 us (52%)
  local copies, waits for them, and re-layouts  150 us (25%)
  blocking collectives  57 us (10%)
  matrix products  33.1 us (6%)
  between operations  14.5 us (2%)
  starting transfers between devices  13.9 us (2%)
  other arithmetic  12.6 us (2%)
    reduce_scatter x1, waiting for transfers between devices, on_device(): lax.psum_scatter(grad_in, 'item', scatter_dimension=0, tiled=True)  90.9 us
    reduce_scatter x1, waiting for transfers between devices, on_device(): lax.psum_scatter(grad_out, 'item', scatter_dimension=0, tiled=True)  70.4 us
    scatter x1, local copies, waits for them, and re-layouts, on_device(): jnp.zeros((owner_count, pos_capacity), jnp.int32).at[pos_owners, pos_slots]  58.5 us
    all_to_all x1, blocking collectives, on_device(): lax.all_to_all(pos_back, 'item', split_axis=0, concat_axis=0, tiled=True)  57 us
    scatter x1, local copies, waits for them, and re-layouts, on_device(): pos_back = jnp.zeros((owner_count, pos_capacity, width), jnp.float32).at[...  49.9 us
    reduce_scatter x1, waiting for transfers between devices, on_device(): lax.psum_scatter(grad_query, 'item', scatter_dimension=0, tiled=True)  47.6 us
    reduce_scatter x1, waiting for transfers between devices, on_device(): lax.psum_scatter(reduced[1], 'query', scatter_dimension=1, tiled=True)  24.7 us
    reduce_scatter x1, waiting for transfers between devices, on_device(): lax.psum_scatter(reduced[0], 'query', scatter_dimension=1, tiled=True)  22.1 us
  transfers between devices with their start and end apart: 10, of which 8 were waited for; matrix products, arithmetic and copies ran while one was open for 18% of the time, Pallas kernels for 0%

commit v1 on v0

v1 whole, which is shorter than its diff:
```python
import functools
import math

import jax
import jax.numpy as jnp
from jax import lax
from jax.experimental import pallas as pl
from jax.experimental.pallas import tpu as pltpu
from jax.sharding import PartitionSpec as P

TAU = 0.02
EPS = 1e-06
CORES = 2
PARTS = 2
DEPTH = 4


def add_tiles(shape, left, right, out):
    count = math.prod(shape)

    def body(step, carry):
        index = []
        rest = step
        for size in reversed(shape):
            index.insert(0, lax.rem(rest, size))
            rest = lax.div(rest, size)
        index = tuple(index)
        total = left(index)[...].astype(jnp.float32) + right(index)[...].astype(jnp.float32)
        out(index)[...] = total.astype(out(index).dtype)
        return carry

    lax.fori_loop(0, count, body, 0)


def reduce_kernel(
    sizes, grads, out, pair, x_first, y_first, y_second, x_second, held_x, held_y, last, total_a, total_b, send, recv
):
    nx, nz, ny = sizes
    query = lax.axis_index("query")
    item = lax.axis_index("item")
    my_x, my_core = query // CORES, query % CORES
    my_z, my_y = item // ny, item % ny

    def at_core(c):
        return {"query": my_x * CORES + c, "item": item}

    def at_x(x):
        return {"query": x * CORES + my_core, "item": item}

    def at_y(y):
        return {"query": query, "item": my_z * ny + y}

    def at_z(z):
        return {"query": query, "item": z * ny + my_y}

    other = 1 - my_core
    xs = [lax.rem(my_x + d, nx) for d in range(1, nx)]
    ys = [lax.rem(my_y + d, ny) for d in range(1, ny)]
    zs = [lax.rem(my_z + d, nz) for d in range(1, nz)]
    barrier = pltpu.get_barrier_semaphore()
    partners = [at_core(other)] + [at_x(x) for x in xs] + [at_y(y) for y in ys] + [at_z(z) for z in zs]
    for partner in partners:
        pl.semaphore_signal(barrier, inc=1, device_id=partner, device_id_type=pl.DeviceIdType.MESH)
    pl.semaphore_wait(barrier, len(partners))

    used = [0]

    def copy(source, target, partner):
        slot = used[0]
        used[0] += 1
        made = pltpu.make_async_remote_copy(
            src_ref=source,
            dst_ref=target,
            send_sem=send.at[slot],
            recv_sem=recv.at[slot],
            device_id=partner,
            device_id_type=pl.DeviceIdType.MESH,
        )
        made.start()
        return made

    core_copies = [
        copy(grads.at[part, :, other], pair.at[part], at_core(other)) for part in range(PARTS)
    ]

    def core_sum(part):
        core_copies[part].wait_recv()
        add_tiles(
            (nx, nz, ny),
            lambda i: grads.at[part, i[0], my_core, i[1], i[2]],
            lambda i: pair.at[part, i[0], i[1], i[2]],
            lambda i: (held_x if part == 0 else held_y).at[i[0], i[1], i[2]],
        )

    core_sum(0)
    a1 = [copy(held_x.at[x], x_first.at[d], at_x(x)) for d, x in enumerate(xs)]
    core_sum(1)
    b1 = [copy(held_y.at[:, :, y], y_first.at[d], at_y(y)) for d, y in enumerate(ys)]

    for d, made in enumerate(a1):
        made.wait_recv()
        base = (lambda i: held_x.at[my_x, i[0], i[1]]) if d == 0 else (lambda i: pair.at[0, 0, i[0], i[1]])
        add_tiles((nz, ny), base, lambda i, d=d: x_first.at[d, i[0], i[1]], lambda i: pair.at[0, 0, i[0], i[1]])
    a2 = [copy(pair.at[0, 0, :, y], y_second.at[d], at_y(y)) for d, y in enumerate(ys)]

    for d, made in enumerate(b1):
        made.wait_recv()
        base = (lambda i: held_y.at[i[0], i[1], my_y]) if d == 0 else (lambda i: pair.at[1, i[0], i[1], 0])
        add_tiles((nx, nz), base, lambda i, d=d: y_first.at[d, i[0], i[1]], lambda i: pair.at[1, i[0], i[1], 0])
    b2 = [copy(pair.at[1, x, :, 0], x_second.at[d], at_x(x)) for d, x in enumerate(xs)]

    for d, made in enumerate(a2):
        made.wait_recv()
        base = (lambda i: pair.at[0, 0, i[0], my_y]) if d == 0 else (lambda i: total_a.at[i[0]])
        add_tiles((nz,), base, lambda i, d=d: y_second.at[d, i[0]], lambda i: total_a.at[i[0]])
    a3 = [copy(total_a.at[z], last.at[0, d], at_z(z)) for d, z in enumerate(zs)]

    for d, made in enumerate(b2):
        made.wait_recv()
        base = (lambda i: pair.at[1, my_x, i[0], 0]) if d == 0 else (lambda i: total_b.at[i[0]])
        add_tiles((nz,), base, lambda i, d=d: x_second.at[d, i[0]], lambda i: total_b.at[i[0]])
    b3 = [copy(total_b.at[z], last.at[1, d], at_z(z)) for d, z in enumerate(zs)]

    for part, copies, total in ((0, a3, total_a), (1, b3, total_b)):
        for made in copies:
            made.wait_recv()
        result = total[my_z].astype(jnp.float32)
        for d in range(nz - 1):
            result = result + last[part, d].astype(jnp.float32)
        out[part] = result
    for made in core_copies + a1 + b1 + a2 + b2 + a3 + b3:
        made.wait_send()


def reduce_grads(grads, sizes):
    nx, nz, ny = sizes
    rows, width = grads.shape[-2:]
    tile = (rows, width)
    copies = PARTS + 2 * (nx - 1) + 2 * (ny - 1) + 2 * (nz - 1)

    def held(*lead):
        return pltpu.VMEM(lead + tile, jnp.bfloat16)

    return pl.pallas_call(
        functools.partial(reduce_kernel, sizes),
        out_shape=jax.ShapeDtypeStruct((PARTS,) + tile, jnp.float32),
        in_specs=[pl.BlockSpec(memory_space=pltpu.VMEM)],
        out_specs=pl.BlockSpec(memory_space=pltpu.VMEM),
        scratch_shapes=[
            held(PARTS, nx, nz, ny),
            held(nx - 1, nz, ny),
            held(ny - 1, nx, nz),
            held(ny - 1, nz),
            held(nx - 1, nz),
            held(nx, nz, ny),
            held(nx, nz, ny),
            held(PARTS, nz - 1),
            held(nz),
            held(nz),
            pltpu.SemaphoreType.DMA((copies,)),
            pltpu.SemaphoreType.DMA((copies,)),
        ],
        compiler_params=pltpu.CompilerParams(
            collective_id=0, has_side_effects=True, vmem_limit_bytes=40 * 1024 * 1024
        ),
        cost_estimate=pl.CostEstimate(flops=10**7, bytes_accessed=10**8, transcendentals=0),
    )(grads)


def slot_numbers(owners):
    place = jnp.arange(owners.shape[0], dtype=jnp.int32)
    same = (owners[:, None] == owners[None, :]) & (place[:, None] < place[None, :])
    return jnp.sum(same.astype(jnp.int32), axis=0)


def pick(flat, rows):
    onehot = (flat[:, None] == jnp.arange(rows.shape[0], dtype=jnp.int32)[None, :]).astype(
        jnp.bfloat16
    )
    return jnp.dot(onehot, rows, preferred_element_type=jnp.float32).astype(jnp.bfloat16)


def to_slots(flat, values, count):
    hit = flat[:, None] == jnp.arange(count, dtype=jnp.int32)[None, :]
    return jnp.sum(jnp.where(hit, values[:, None], 0), axis=0)


def item_tower(features, w_item_in, w_item_out):
    hidden_pre = jnp.dot(features, w_item_in, preferred_element_type=jnp.float32)
    hidden = jax.nn.silu(hidden_pre).astype(jnp.bfloat16)
    output = jnp.dot(hidden, w_item_out, preferred_element_type=jnp.float32)
    inverse = lax.rsqrt(jnp.sum(output * output, axis=-1, keepdims=True) + EPS)
    unit = output * inverse
    return (hidden_pre, hidden, inverse, unit, unit.astype(jnp.bfloat16))


def tower_grads(features, hidden_pre, hidden, inverse, unit, upstream, w_item_out):
    out_grad = (
        inverse * (upstream - unit * jnp.sum(unit * upstream, axis=-1, keepdims=True))
    ).astype(jnp.bfloat16)
    hidden_grad = lax.dot_general(
        out_grad, w_item_out, (((1,), (1,)), ((), ())), preferred_element_type=jnp.float32
    )
    sigma = jax.nn.sigmoid(hidden_pre)
    pre_grad = (hidden_grad * (sigma * (1.0 + hidden_pre * (1.0 - sigma)))).astype(jnp.bfloat16)
    grad_out = lax.dot_general(
        hidden, out_grad, (((0,), (0,)), ((), ())), preferred_element_type=jnp.float32
    )
    grad_in = lax.dot_general(
        features, pre_grad, (((0,), (0,)), ((), ())), preferred_element_type=jnp.float32
    )
    return (grad_in, grad_out)


def on_device(
    queries,
    item_table,
    w_query,
    w_item_in,
    w_item_out,
    pos_owner,
    pos_rows,
    neg_owner,
    neg_rows,
    neg_logq,
):
    owner_count = lax.axis_size("item")
    query_axis = lax.axis_size("query")
    query_count = queries.shape[0]
    total_queries = query_count * owner_count * query_axis
    loss_scale = 1.0 / math.sqrt(total_queries)
    my_index = lax.axis_index("item")
    negatives = neg_rows.shape[1]
    capacity = 2 * (negatives // owner_count)
    pos_capacity = max(2, 2 * query_count // owner_count)

    pos_owners = pos_owner[:, 0]
    pos_flat = pos_owners * pos_capacity + slot_numbers(pos_owners)
    request = to_slots(pos_flat, pos_rows, owner_count * pos_capacity)
    asked = lax.all_to_all(
        request.reshape(owner_count, pos_capacity), "item", split_axis=0, concat_axis=0, tiled=True
    )
    neg_owners = neg_owner[0, :, 0]
    neg_flat = neg_owners * capacity + slot_numbers(neg_owners)
    own_rows = to_slots(neg_flat - my_index * capacity, neg_rows[0], capacity)

    neg_own = jnp.take(item_table, own_rows, axis=0, mode="clip")
    neg_held = lax.all_gather(neg_own, "item", axis=0, tiled=True)
    pos_own = jnp.take(item_table, asked.reshape(-1), axis=0, mode="clip")
    pos_held = lax.all_to_all(
        pos_own.reshape(owner_count, pos_capacity, -1), "item", split_axis=0, concat_axis=0, tiled=True
    ).reshape(owner_count * pos_capacity, -1)

    query_pre = jnp.dot(queries, w_query, preferred_element_type=jnp.float32)
    query_scale = lax.rsqrt(jnp.sum(query_pre * query_pre, axis=-1, keepdims=True) + EPS)
    query_unit = query_pre * query_scale
    query_embed = query_unit.astype(jnp.bfloat16)

    features = jnp.concatenate([pick(neg_flat, neg_held), pick(pos_flat, pos_held)], axis=0)
    hidden_pre, hidden, inverse, unit, item_embed = item_tower(features, w_item_in, w_item_out)
    neg_embed = item_embed[:negatives]
    pos_embed = item_embed[negatives:]
    scores = lax.dot_general(
        query_embed, neg_embed, (((1,), (1,)), ((), ())), preferred_element_type=jnp.float32
    )
    weights_exp = jnp.exp(scores / TAU - neg_logq)
    pos_logit = (
        jnp.sum(query_embed.astype(jnp.float32) * pos_embed.astype(jnp.float32), axis=-1) / TAU
    )
    pos_exp = jnp.exp(pos_logit)
    total = pos_exp + jnp.sum(weights_exp, axis=-1)
    neg_weight = (loss_scale * weights_exp / total[:, None]).astype(jnp.bfloat16)
    pos_weight = loss_scale * (pos_exp / total - 1.0)
    query_grad = (
        jnp.dot(neg_weight, neg_embed, preferred_element_type=jnp.float32)
        + pos_weight[:, None] * pos_embed.astype(jnp.float32)
    ) / TAU
    pre_grad_query = (
        query_scale
        * (query_grad - query_unit * jnp.sum(query_unit * query_grad, axis=-1, keepdims=True))
    ).astype(jnp.bfloat16)
    grad_query = lax.dot_general(
        queries, pre_grad_query, (((0,), (0,)), ((), ())), preferred_element_type=jnp.float32
    )
    pos_grad = pos_weight[:, None] * query_embed.astype(jnp.float32) / TAU
    neg_grad = (
        lax.dot_general(
            neg_weight, query_embed, (((0,), (0,)), ((), ())), preferred_element_type=jnp.float32
        )
        / TAU
    )
    upstream = jnp.concatenate([neg_grad, pos_grad], axis=0)
    grad_in, grad_out = tower_grads(
        features, hidden_pre, hidden, inverse, unit, upstream, w_item_out
    )

    nz = DEPTH if owner_count % DEPTH == 0 else 1
    ny = owner_count // nz
    nx = query_axis // CORES

    def blocks(grad):
        rows = grad.shape[0] // (owner_count * PARTS)
        split = grad.astype(jnp.bfloat16).reshape(nz, ny, PARTS, rows, nx, CORES, -1)
        return split.transpose(2, 4, 5, 0, 1, 3, 6)

    widths = [grad.shape[1] // query_axis for grad in (grad_query, grad_in, grad_out)]
    grads = jnp.concatenate([blocks(grad_query), blocks(grad_in), blocks(grad_out)], axis=-1)
    summed = reduce_grads(grads, (nx, nz, ny)).reshape(-1, grads.shape[-1])
    return (
        summed[:, : widths[0]],
        summed[:, widths[0] : widths[0] + widths[1]],
        summed[:, widths[0] + widths[1] :],
    )


def solution(mesh):
    return jax.shard_map(
        on_device,
        mesh=mesh,
        in_specs=(
            P(("query", "item"), None),
            P("item", None),
            P(),
            P(),
            P(),
            P(("query", "item"), None),
            P(("query", "item")),
            P("query", None, None),
            P("query", None),
            P("query", None),
        ),
        out_specs=(P("item", "query"), P("item", "query"), P("item", "query")),
        check_vma=False,
    )
```

time: 598 us -> 227 us (0.38)
  waiting for transfers between devices: 313 us -> 67.9 us
  local copies, waits for them, and re-layouts: 150 us -> 36.2 us
  blocking collectives: 57 us -> 13.5 us
  Pallas kernels: 0 us -> 39.3 us
  starting transfers between devices: 13.9 us -> 4.51 us
  matrix products: 33.1 us -> 40.1 us
    reduce_scatter x7 -> x0, waiting for transfers between devices: 277 us -> none  [the longest x1 90.9 us: on_device(): lax.psum_scatter(grad_in, 'item', scatter_dimension=0, tiled=True)]
    scatter x3 -> x0, local copies, waits for them, and re-layouts: 108 us -> none  [the longest x1 58.5 us: on_device(): jnp.zeros((owner_count, pos_capacity), jnp.int32).at[pos_owners, pos_slots]]
    all_to_all x1, blocking collectives: 57 us -> 13.5 us  [on_device(): lax.all_to_all(request.reshape(owner_count, pos_capacity), 'item', split_...]
    all_to_all x2 -> x1, waiting for transfers between devices: 16.1 us -> 57.7 us  [on_device(): lax.all_to_all(pos_own.reshape(owner_count, pos_capacity, -1), 'item', sp...]
    pallas_call x0 -> x1, Pallas kernels: none -> 39.3 us  [reduce_grads(): pl.pallas_call(functools.partial(reduce_kernel, sizes), out_shape=jax.Sha...]
    unnamed x41 -> x28, local copies, waits for them, and re-layouts: 21.6 us -> 0.73 us
    reshape x2 -> x6, local copies, waits for them, and re-layouts: 0.15 us -> 17.7 us  [blocks(): grad.astype(jnp.bfloat16).reshape(nz, ny, PARTS, rows, nx, CORES, -1)]
    dot_general x0 -> x2, matrix products: none -> 10.3 us  [pick(): jnp.dot(onehot, rows, preferred_element_type=jnp.float32)]
  transfers between devices with their start and end apart: 10 -> 2, of which waited for: 8 -> 2; matrix products, arithmetic and copies ran while one was open for 18% -> 6% of each run, Pallas kernels for 0% -> 0%
where the time goes in v1:
time: 227 us
  waiting for transfers between devices  67.9 us (30%)
  matrix products  40.1 us (18%)
  Pallas kernels  39.3 us (17%)
  local copies, waits for them, and re-layouts  36.2 us (16%)
  between operations  14.3 us (6%)
  blocking collectives  13.5 us (6%)
  other arithmetic  10.9 us (5%)
  starting transfers between devices  4.51 us (2%)
    all_to_all x1, waiting for transfers between devices, on_device(): lax.all_to_all(pos_own.reshape(owner_count, pos_capacity, -1), 'item', sp...  57.7 us
    pallas_call x1, Pallas kernels, reduce_grads(): pl.pallas_call(functools.partial(reduce_kernel, sizes), out_shape=jax.Sha...  39.3 us
    reshape x6, local copies, waits for them, and re-layouts, blocks(): grad.astype(jnp.bfloat16).reshape(nz, ny, PARTS, rows, nx, CORES, -1)  17.7 us
    all_to_all x1, blocking collectives, on_device(): lax.all_to_all(request.reshape(owner_count, pos_capacity), 'item', split_...  13.5 us
    dot_general x1, matrix products, tower_grads(): lax.dot_general(features, pre_grad, (((0,), (0,)), ((), ())), preferred_e...  10.8 us
    dot_general x2, matrix products, pick(): jnp.dot(onehot, rows, preferred_element_type=jnp.float32)  10.3 us
    all_gather x1, waiting for transfers between devices, on_device(): neg_held = lax.all_gather(neg_own, 'item', axis=0, tiled=True)  10.2 us
    gather x1, local copies, waits for them, and re-layouts, on_device(): pos_own = jnp.take(item_table, asked.reshape(-1), axis=0, mode='clip')  7.31 us
  transfers between devices with their start and end apart: 2, of which 2 were waited for; matrix products, arithmetic and copies ran while one was open for 6% of the time, Pallas kernels for 0%

profile of v1, /device:TPU:0, one launch (start us, length us, event | category | flops | bytes accessed | tf_op | source)
XLA Modules:
  0.0 226.7 jit_solution(8666873990109052526)
XLA Ops:
  10.2 5.1 %gather_fusion = bf16[256,1024]{1,0:T(8,128)(2,1)} fusion(bf16[2048,1024]{1,0:T(8,128)(2,1)} %param.11, s32[1024]{0:T(1024)S(1)} %pad_clamp_fusion.1), kind=kCustom, calls=%fused_computation | custom fusion | bytes 1049600 | tf_op jit(solution)/shard_map/jit(_take)/gather | solution.py:247
  15.8 13.5 %all_to_all.14 = s32[8,1,96]{2,1,0:T(1,128)S(1)} all-to-all(s32[8,1,96]{2,1,0:T(1,128)S(1)} %all_to_all.9), channel_id=1, replica_groups=mesh['query'=4,'item'=8] {'item'}, dimensions={0} | all-to-all | bytes 6144 | tf_op jit(solution)/shard_map/all_to_all | solution.py:240
  30.6 7.3 %gather_fusion.1 = bf16[768,1024]{1,0:T(8,128)(2,1)} fusion(bf16[2048,1024]{1,0:T(8,128)(2,1)} %param.11, s32[1024]{0:T(1024)S(1)} %pad_clamp_fusion), kind=kCustom, calls=%fused_computation.1 | custom fusion | bytes 3148800 | tf_op jit(solution)/shard_map/jit(_take)/gather | solution.py:249
  37.9 4.5 %all-to-all-start.1 = ((bf16[8,96,1024]{2,1,0:T(8,128)(2,1)}), bf16[8,96,1024]{2,1,0:T(8,128)(2,1)}, u32[]{:S(2)}, u32[]{:S(2)}) async-start(bf16[8,96,1024]{2,1,0:T(8,128)(2,1)} %bitcast.34), calls=%async_computation.1 | async-start | bytes 3145728 | tf_op jit(solution)/shard_map/all_to_all | solution.py:250
  42.4 2.1 multiply_reduce_fusion.3
  44.6 57.7 %all-to-all-done.1 = bf16[8,96,1024]{2,1,0:T(8,128)(2,1)} async-done(((bf16[8,96,1024]{2,1,0:T(8,128)(2,1)}), bf16[8,96,1024]{2,1,0:T(8,128)(2,1)}, u32[]{:S(2)}, u32[]{:S(2)}) %all-to-all-start.1) | async-done | bytes 1572896 | tf_op jit(solution)/shard_map/all_to_all | solution.py:250
  102.2 3.1 %convolution_convert_fusion.2 = bf16[384,1024]{1,0:T(8,128)(2,1)} fusion(bf16[768,1024]{1,0:T(8,128)(2,1)} %bitcast.3, s32[384]{0:T(512)S(1)} %add_reduce_fusion), kind=kOutput, calls=%fused_computation.28 | convolution fusion | flops 604667904 | bytes 2360832 | tf_op jit(solution)/shard_map/dot_general | solution.py:180
  105.4 10.2 %all-gather.3.cloned.1.call-done = bf16[2048,1024]{1,0:T(8,128)(2,1)} async-done(((bf16[256,1024]{1,0:T(8,128)(2,1)}), bf16[2048,1024]{1,0:T(8,128)(2,1)}) %all-gather.3.cloned.1.call-update) | async-done | bytes 4194320 | tf_op jit(solution)/shard_map/all_gather | solution.py:248
  115.6 7.1 %fusion.4 = bf16[1024,1024]{1,0:T(8,128)(2,1)S(1)} fusion(bf16[2048,1024]{1,0:T(8,128)(2,1)} %all-gather.3.cloned.1.call-done, s32[1024]{0:T(1024)S(1)} %get-tuple-element.6), kind=kOutput, calls=%fused_computation.20 | convolution fusion | flops 4298113024 | bytes 6295552 | tf_op jit(solution)/shard_map/dot_general | solution.py:180
  122.7 6.4 %multiply_convert_fusion.1 = (bf16[1408,1024]{1,0:T(8,128)(2,1)S(1)}, f32[1408,1024]{1,0:T(8,128)}) fusion(bf16[1024,1024]{1,0:T(8,128)(2,1)S(1)} %copy-done, bf16[384,1024]{1,0:T(8,128)(2,1)S(1)} %copy-done.10, bf16[1024,1024]{1,0:T(8,128)(2,1)S(1)} %fusion.4), kind=kOutput, calls=%fused_computation.5 | convolution fusion | flops 2965766144 | bytes 13631488 | tf_op jit(solution)/shard_map/dot_general | solution.py:189
  129.1 3.6 %multiply_reduce_fusion.1 = (f32[1408]{0:T(1024)S(1)}, f32[1408,512]{0,1:T(8,128)}) fusion(bf16[1408,1024]{1,0:T(8,128)(2,1)S(1)} %get-tuple-element.11, bf16[1024,512]{1,0:T(8,128)(2,1)S(1)} %copy-done.8), kind=kOutput, calls=%fused_computation.16 | convolution fusion | flops 1477835392 | bytes 6821376 | tf_op jit(solution)/shard_map/dot_general | solution.py:191
  132.7 3.5 %copy.19 = f32[1408,512]{1,0:T(8,128)} copy(f32[1408,512]{0,1:T(8,128)} %get-tuple-element.14) | data formatting | bytes 5767168 | tf_op jit(solution)/shard_map/dot_general | solution.py:191
  136.2 2.1 multiply_convert_fusion.3
  140.2 1.6 multiply_reduce_fusion.2
  142.9 1.5 multiply_convert_fusion.2
  144.7 2.9 %convolution_convert_fusion = bf16[1024,512]{1,0:T(8,128)(2,1)} fusion(bf16[1408,1024]{1,0:T(8,128)(2,1)S(1)} %copy-done.12, bf16[1408,512]{1,0:T(8,128)(2,1)S(1)} %multiply_convert_fusion.2), kind=kOutput, calls=%fused_computation.26 | convolution fusion | flops 1476919296 | bytes 5373952 | tf_op jit(solution)/shard_map/dot_general | solution.py:206
  147.6 10.8 %fusion.5 = bf16[1024,1024]{1,0:T(8,128)(2,1)} fusion(f32[1408,1024]{1,0:T(8,128)} %get-tuple-element.12, bf16[1408,512]{1,0:T(8,128)(2,1)S(1)} %multiply_convert_fusion.2, bf16[1024,512]{1,0:T(8,128)(2,1)} %param.14, bf16[384,1024]{1,0:T(8,128)(2,1)} %convolution_convert_fusion.2, bf16[1024,1024]{1,0:T(8,128)(2,1)} %copy-done.13), kind=kOutput, calls=%fused_computation.21 | convolution fusion | flops 4448976896 | bytes 13238272 | tf_op jit(solution)/shard_map/dot_general | solution.py:209
  158.4 1.3 reshape.83
  161.0 4.5 %reshape.82 = bf16[4,2,2,64,2,2,256]{6,5,4,3,2,1,0:T(2,128)(2,1)} reshape(bf16[1024,1024]{1,0:T(8,128)(2,1)} %fusion.5) | data formatting | bytes 4194304 | tf_op jit(solution)/shard_map/reshape | solution.py:303
  165.5 3.5 %copy.28 = bf16[4,2,2,64,2,2,256]{6,3,1,0,5,4,2:T(8,128)(2,1)} copy(bf16[4,2,2,64,2,2,256]{6,5,4,3,2,1,0:T(2,128)(2,1)} %reshape.82) | data formatting | bytes 4194304 | tf_op jit(solution)/shard_map/reshape | solution.py:303
  169.9 2.3 %reshape.104 = bf16[4,2,2,64,2,2,128]{3,2,1,0,6,5,4:T(2,128)(2,1)} reshape(bf16[1024,512]{0,1:T(8,128)(2,1)S(1)} %fusion.7) | data formatting | bytes 2097152 | tf_op jit(solution)/shard_map/reshape | solution.py:303
  172.2 4.8 %copy.21 = bf16[4,2,2,64,2,2,128]{6,3,1,0,5,4,2:T(8,128)(2,1)S(1)} copy(bf16[4,2,2,64,2,2,128]{3,2,1,0,6,5,4:T(2,128)(2,1)} %reshape.104) | data formatting | bytes 2097152 | tf_op jit(solution)/shard_map/reshape | solution.py:303
  177.0 2.2 pad_maximum_fusion.grads
  179.3 39.3 %shard_map.121 = f32[2,64,512]{2,1,0:T(8,128)S(1)} custom-call(bf16[2,2,2,4,2,64,512]{6,5,4,3,2,1,0:T(8,128)(2,1)S(1)} %pad_maximum_fusion.grads), custom_call_target="tpu_custom_call" | custom-call | flops 10000000 | bytes 100000000 | tf_op jit(solution)/shard_map/pallas_call | solution.py:144
  (55 shorter events, 11.6 us)
Async XLA Ops:
  7.2 115.5 %copy-start = (bf16[1024,1024]{1,0:T(8,128)(2,1)S(1)}, bf16[1024,1024]{1,0:T(8,128)(2,1)}, u32[]{:S(2)}) copy-start(bf16[1024,1024]{1,0:T(8,128)(2,1)} %param.13) | copy-start | bytes 6291460
  7.2 8.2 %copy-start.6 = (s32[384,1]{0,1:T(1,128)S(1)}, s32[384,1]{0,1:T(1,128)}, u32[]{:S(2)}) copy-start(s32[384,1]{0,1:T(1,128)} %param.15) | copy-start | bytes 4612
  7.2 8.4 %copy-start.7 = (s32[384]{0:T(512)S(1)}, s32[384]{0:T(512)}, u32[]{:S(2)}) copy-start(s32[384]{0:T(512)} %param.16) | copy-start | bytes 4612
  7.2 108.4 %all-gather.3.cloned.1.call-start = ((), (), s32[]{:S(2)}) async-start(), calls=%async_computation.2 | async-start | bytes 4718592 | tf_op jit(solution)/shard_map/all_gather | solution.py:248
  37.9 64.3 %all-to-all-start.1 = ((bf16[8,96,1024]{2,1,0:T(8,128)(2,1)}), bf16[8,96,1024]{2,1,0:T(8,128)(2,1)}, u32[]{:S(2)}, u32[]{:S(2)}) async-start(bf16[8,96,1024]{2,1,0:T(8,128)(2,1)} %bitcast.34), calls=%async_computation.1 | async-start | bytes 3145728 | tf_op jit(solution)/shard_map/all_to_all | solution.py:250
  44.5 95.6 %copy-start.2 = (f32[384,512]{1,0:T(8,128)}, f32[384,512]{1,0:T(8,128)S(1)}, u32[]{:S(2)}) copy-start(f32[384,512]{1,0:T(8,128)S(1)} %get-tuple-element.16) | copy-start | bytes 2359300
  115.6 7.2 %copy-start.10 = (bf16[384,1024]{1,0:T(8,128)(2,1)S(1)}, bf16[384,1024]{1,0:T(8,128)(2,1)}, u32[]{:S(2)}) copy-start(bf16[384,1024]{1,0:T(8,128)(2,1)} %convolution_convert_fusion.2) | copy-start | bytes 2359300
  122.7 6.4 %copy-start.13 = (bf16[1024,1024]{1,0:T(8,128)(2,1)}, bf16[1024,1024]{1,0:T(8,128)(2,1)S(1)}, u32[]{:S(2)}) copy-start(bf16[1024,1024]{1,0:T(8,128)(2,1)S(1)} %fusion.4) | copy-start | bytes 6291460
  122.7 6.4 %copy-start.8 = (bf16[1024,512]{1,0:T(8,128)(2,1)S(1)}, bf16[1024,512]{1,0:T(8,128)(2,1)}, u32[]{:S(2)}) copy-start(bf16[1024,512]{1,0:T(8,128)(2,1)} %param.14) | copy-start | bytes 3145732
  129.1 3.6 %copy-start.11 = (bf16[1408,1024]{1,0:T(8,128)(2,1)}, bf16[1408,1024]{1,0:T(8,128)(2,1)S(1)}, u32[]{:S(2)}) copy-start(bf16[1408,1024]{1,0:T(8,128)(2,1)S(1)} %get-tuple-element.11) | copy-start | bytes 8650756
  136.2 2.4 %copy-start.9 = (f32[1,1024]{1,0:T(1,128)S(1)}, f32[1,1024]{1,0:T(1,128)}, u32[]{:S(2)}) copy-start(f32[1,1024]{1,0:T(1,128)} %param.19) | copy-start | bytes 12292
  140.2 2.1 copy-start.1
  142.9 1.8 copy-start.12
  165.5 3.5 %copy-start.3 = (f32[384,512]{1,0:T(8,128)S(1)}, f32[384,512]{1,0:T(8,128)}, u32[]{:S(2)}) copy-start(f32[384,512]{1,0:T(8,128)} %copy-done.2) | copy-start | bytes 2359300
  165.5 3.5 %copy-start.4 = (bf16[384,1024]{1,0:T(8,128)(2,1)S(1)}, bf16[384,1024]{1,0:T(8,128)(2,1)}, u32[]{:S(2)}) copy-start(bf16[384,1024]{1,0:T(8,128)(2,1)} %param.10) | copy-start | bytes 2359300
  165.5 3.5 %copy-start.5 = (f32[384,512]{1,0:T(8,128)S(1)}, f32[384,512]{1,0:T(8,128)}, u32[]{:S(2)}) copy-start(f32[384,512]{1,0:T(8,128)} %get-tuple-element.20) | copy-start | bytes 2359300
Sparse Core Ops, SparseCore 0:
  15.5 100.0 all-gather.2

commit v2 on v1

--- a/solution.py
+++ b/solution.py
@@ -13,6 +13,7 @@
 CORES = 2
 PARTS = 2
 DEPTH = 4
+TILE = 256
 
 
 def add_tiles(shape, left, right, out):
@@ -33,7 +34,8 @@
 
 
 def reduce_kernel(
-    sizes, grads, out, pair, x_first, y_first, y_second, x_second, held_x, held_y, last, total_a, total_b, send, recv
+    sizes, queries, features, hidden, query_side, in_side, out_side, out, grads, pair, x_first, y_first, y_second, x_second,
+    held_x, held_y, last, total_a, total_b, send, recv
 ):
     nx, nz, ny = sizes
     query = lax.axis_index("query")
@@ -79,9 +81,41 @@
         made.start()
         return made
 
+    rows = grads.shape[-2]
+    span = rows * PARTS
+    items = TILE // span
+
+    def products(core):
+        def body(tile, carry):
+            here = pl.ds(pl.multiple_of(tile * TILE, TILE), TILE)
+            made = []
+            for left, right in ((queries, query_side), (features, in_side), (hidden, out_side)):
+                made.append(
+                    lax.dot_general(
+                        left[:, here],
+                        right[core],
+                        (((0,), (0,)), ((), ())),
+                        preferred_element_type=jnp.float32,
+                    ).astype(jnp.bfloat16)
+                )
+            for x in range(nx):
+                block = jnp.concatenate(
+                    [m[:, x * (m.shape[1] // nx) : (x + 1) * (m.shape[1] // nx)] for m in made], axis=1
+                )
+                for j in range(items):
+                    place = tile * items + j
+                    for part in range(PARTS):
+                        start = j * span + part * rows
+                        grads[part, x, core, place // ny, place % ny] = block[start : start + rows]
+            return carry
+
+        lax.fori_loop(0, queries.shape[1] // TILE, body, 0)
+
+    products(other)
     core_copies = [
         copy(grads.at[part, :, other], pair.at[part], at_core(other)) for part in range(PARTS)
     ]
+    products(my_core)
 
     def core_sum(part):
         core_copies[part].wait_recv()
@@ -132,10 +166,8 @@
         made.wait_send()
 
 
-def reduce_grads(grads, sizes):
+def reduce_grads(operands, sizes, tile):
     nx, nz, ny = sizes
-    rows, width = grads.shape[-2:]
-    tile = (rows, width)
     copies = PARTS + 2 * (nx - 1) + 2 * (ny - 1) + 2 * (nz - 1)
 
     def held(*lead):
@@ -144,9 +176,10 @@
     return pl.pallas_call(
         functools.partial(reduce_kernel, sizes),
         out_shape=jax.ShapeDtypeStruct((PARTS,) + tile, jnp.float32),
-        in_specs=[pl.BlockSpec(memory_space=pltpu.VMEM)],
+        in_specs=[pl.BlockSpec(memory_space=pltpu.VMEM)] * len(operands),
         out_specs=pl.BlockSpec(memory_space=pltpu.VMEM),
         scratch_shapes=[
+            held(PARTS, nx, CORES, nz, ny),
             held(PARTS, nx, nz, ny),
             held(nx - 1, nz, ny),
             held(ny - 1, nx, nz),
@@ -163,8 +196,134 @@
         compiler_params=pltpu.CompilerParams(
             collective_id=0, has_side_effects=True, vmem_limit_bytes=40 * 1024 * 1024
         ),
-        cost_estimate=pl.CostEstimate(flops=10**7, bytes_accessed=10**8, transcendentals=0),
-    )(grads)
+        cost_estimate=pl.CostEstimate(flops=10**10, bytes_accessed=10**7, transcendentals=0),
+    )(*operands)
+
+
+def fetch_kernel(sizes, neg_own, pos_own, neg_out, pos_out, z_send, z_recv, y_send, y_recv, p_send, p_recv):
+    nz, ny = sizes
+    item_count = nz * ny
+    item = lax.axis_index("item")
+    my_z, my_y = item // ny, item % ny
+    peers = [lax.rem(item + d, item_count) for d in range(1, item_count)]
+    barrier = pltpu.get_barrier_semaphore()
+    for peer in peers:
+        pl.semaphore_signal(
+            barrier, inc=1, device_id={"item": peer}, device_id_type=pl.DeviceIdType.MESH
+        )
+    pl.semaphore_wait(barrier, len(peers))
+
+    def copy(source, target, send, recv, peer):
+        return pltpu.make_async_remote_copy(
+            src_ref=source,
+            dst_ref=target,
+            send_sem=send,
+            recv_sem=recv,
+            device_id={"item": peer},
+            device_id_type=pl.DeviceIdType.MESH,
+        )
+
+    def along_z(way, step, block):
+        source = neg_own if step == 0 else neg_out.at[block * ny + my_y]
+        to = (my_z + (1 if way == 0 else -1) + nz) % nz
+        return copy(
+            source, neg_out.at[block * ny + my_y], z_send.at[way, step], z_recv.at[way, step], to * ny + my_y
+        )
+
+    def along_y(way, step, d, block):
+        source = neg_own if step == 0 else neg_out.at[block * ny + my_y]
+        to = my_z * ny + lax.rem(my_y + d, ny)
+        return copy(
+            source, neg_out.at[block * ny + my_y], y_send.at[way, step, d - 1], y_recv.at[way, step, d - 1], to
+        )
+
+    def from_y(way, step, d, block):
+        other = lax.rem(my_y + ny - d, ny)
+        return copy(
+            neg_own, neg_out.at[block * ny + other], y_send.at[way, step, d - 1], y_recv.at[way, step, d - 1],
+            my_z * ny + other,
+        )
+
+    def block_at(way, step):
+        block = my_z - step if way == 0 else my_z + step
+        return block, (block >= 0 if way == 0 else block < nz)
+
+    def has_next(way):
+        return my_z < nz - 1 if way == 0 else my_z > 0
+
+    for way in range(2):
+        if nz > 1:
+            pl.when(has_next(way))(lambda way=way: along_z(way, 0, my_z).start())
+    for d in range(1, ny):
+        along_y(0, 0, d, my_z).start()
+    straight = [
+        copy(pos_own.at[peer], pos_out.at[item], p_send.at[d], p_recv.at[d], peer)
+        for d, peer in enumerate(peers)
+    ]
+    for made in straight:
+        made.start()
+    neg_out[item] = neg_own[...]
+    pos_out[item] = pos_own[item]
+    for step in range(1, nz):
+        for way in range(2):
+            block, there = block_at(way, step)
+
+            def arrived(way=way, step=step, block=block):
+                along_z(way, step - 1, block).wait_recv()
+                if step < nz - 1:
+                    pl.when(has_next(way))(lambda: along_z(way, step, block).start())
+                for d in range(1, ny):
+                    along_y(way, step, d, block).start()
+
+            pl.when(there)(arrived)
+    for made in straight:
+        made.wait_recv()
+    for d in range(1, ny):
+        from_y(0, 0, d, my_z).wait_recv()
+        along_y(0, 0, d, my_z).wait_send()
+    for way in range(2):
+        if nz > 1:
+            pl.when(has_next(way))(lambda way=way: along_z(way, 0, my_z).wait_send())
+        for step in range(1, nz):
+            block, there = block_at(way, step)
+
+            def finished(way=way, step=step, block=block):
+                if step < nz - 1:
+                    pl.when(has_next(way))(lambda: along_z(way, step, block).wait_send())
+                for d in range(1, ny):
+                    from_y(way, step, d, block).wait_recv()
+                    along_y(way, step, d, block).wait_send()
+
+            pl.when(there)(finished)
+    for made in straight:
+        made.wait_send()
+
+
+def fetch(neg_own, pos_own, sizes):
+    nz, ny = sizes
+    item_count = nz * ny
+    steps, fans = nz, max(1, ny - 1)
+    return pl.pallas_call(
+        functools.partial(fetch_kernel, sizes),
+        out_shape=(
+            jax.ShapeDtypeStruct((item_count,) + neg_own.shape, neg_own.dtype),
+            jax.ShapeDtypeStruct(pos_own.shape, pos_own.dtype),
+        ),
+        in_specs=[pl.BlockSpec(memory_space=pltpu.VMEM)] * 2,
+        out_specs=(pl.BlockSpec(memory_space=pltpu.VMEM),) * 2,
+        scratch_shapes=[
+            pltpu.SemaphoreType.DMA((2, steps)),
+            pltpu.SemaphoreType.DMA((2, steps)),
+            pltpu.SemaphoreType.DMA((2, steps, fans)),
+            pltpu.SemaphoreType.DMA((2, steps, fans)),
+            pltpu.SemaphoreType.DMA((item_count - 1,)),
+            pltpu.SemaphoreType.DMA((item_count - 1,)),
+        ],
+        compiler_params=pltpu.CompilerParams(
+            collective_id=1, has_side_effects=True, vmem_limit_bytes=32 * 1024 * 1024
+        ),
+        cost_estimate=pl.CostEstimate(flops=10**6, bytes_accessed=10**8, transcendentals=0),
+    )(neg_own, pos_own)
 
 
 def slot_numbers(owners):
@@ -194,7 +353,7 @@
     return (hidden_pre, hidden, inverse, unit, unit.astype(jnp.bfloat16))
 
 
-def tower_grads(features, hidden_pre, hidden, inverse, unit, upstream, w_item_out):
+def tower_grads(hidden_pre, inverse, unit, upstream, w_item_out):
     out_grad = (
         inverse * (upstream - unit * jnp.sum(unit * upstream, axis=-1, keepdims=True))
     ).astype(jnp.bfloat16)
@@ -203,13 +362,7 @@
     )
     sigma = jax.nn.sigmoid(hidden_pre)
     pre_grad = (hidden_grad * (sigma * (1.0 + hidden_pre * (1.0 - sigma)))).astype(jnp.bfloat16)
-    grad_out = lax.dot_general(
-        hidden, out_grad, (((0,), (0,)), ((), ())), preferred_element_type=jnp.float32
-    )
-    grad_in = lax.dot_general(
-        features, pre_grad, (((0,), (0,)), ((), ())), preferred_element_type=jnp.float32
-    )
-    return (grad_in, grad_out)
+    return (pre_grad, out_grad)
 
 
 def on_device(
@@ -245,11 +398,13 @@
     own_rows = to_slots(neg_flat - my_index * capacity, neg_rows[0], capacity)
 
     neg_own = jnp.take(item_table, own_rows, axis=0, mode="clip")
-    neg_held = lax.all_gather(neg_own, "item", axis=0, tiled=True)
     pos_own = jnp.take(item_table, asked.reshape(-1), axis=0, mode="clip")
-    pos_held = lax.all_to_all(
-        pos_own.reshape(owner_count, pos_capacity, -1), "item", split_axis=0, concat_axis=0, tiled=True
-    ).reshape(owner_count * pos_capacity, -1)
+    nz = DEPTH if owner_count % DEPTH == 0 else 1
+    ny = owner_count // nz
+    nx = query_axis // CORES
+    neg_held, pos_held = fetch(neg_own, pos_own.reshape(owner_count, pos_capacity, -1), (nz, ny))
+    neg_held = neg_held.reshape(owner_count * capacity, -1)
+    pos_held = pos_held.reshape(owner_count * pos_capacity, -1)
 
     query_pre = jnp.dot(queries, w_query, preferred_element_type=jnp.float32)
     query_scale = lax.rsqrt(jnp.sum(query_pre * query_pre, axis=-1, keepdims=True) + EPS)
@@ -279,9 +434,6 @@
         query_scale
         * (query_grad - query_unit * jnp.sum(query_unit * query_grad, axis=-1, keepdims=True))
     ).astype(jnp.bfloat16)
-    grad_query = lax.dot_general(
-        queries, pre_grad_query, (((0,), (0,)), ((), ())), preferred_element_type=jnp.float32
-    )
     pos_grad = pos_weight[:, None] * query_embed.astype(jnp.float32) / TAU
     neg_grad = (
         lax.dot_general(
@@ -290,22 +442,16 @@
         / TAU
     )
     upstream = jnp.concatenate([neg_grad, pos_grad], axis=0)
-    grad_in, grad_out = tower_grads(
-        features, hidden_pre, hidden, inverse, unit, upstream, w_item_out
-    )
-
-    nz = DEPTH if owner_count % DEPTH == 0 else 1
-    ny = owner_count // nz
-    nx = query_axis // CORES
-
-    def blocks(grad):
-        rows = grad.shape[0] // (owner_count * PARTS)
-        split = grad.astype(jnp.bfloat16).reshape(nz, ny, PARTS, rows, nx, CORES, -1)
-        return split.transpose(2, 4, 5, 0, 1, 3, 6)
-
-    widths = [grad.shape[1] // query_axis for grad in (grad_query, grad_in, grad_out)]
-    grads = jnp.concatenate([blocks(grad_query), blocks(grad_in), blocks(grad_out)], axis=-1)
-    summed = reduce_grads(grads, (nx, nz, ny)).reshape(-1, grads.shape[-1])
+    in_grad, out_grad = tower_grads(hidden_pre, inverse, unit, upstream, w_item_out)
+
+    def by_core(right):
+        split = right.reshape(right.shape[0], nx, CORES, -1)
+        return split.transpose(2, 0, 1, 3).reshape(CORES, right.shape[0], -1)
+
+    widths = [right.shape[1] // query_axis for right in (pre_grad_query, in_grad, out_grad)]
+    tile = (queries.shape[1] // (owner_count * PARTS), sum(widths))
+    operands = (queries, features, hidden, by_core(pre_grad_query), by_core(in_grad), by_core(out_grad))
+    summed = reduce_grads(operands, (nx, nz, ny), tile).reshape(-1, sum(widths))
     return (
         summed[:, : widths[0]],
         summed[:, widths[0] : widths[0] + widths[1]],

time: 227 us -> 244 us (1.075)
  Pallas kernels: 39.3 us -> 124 us
  waiting for transfers between devices: 67.9 us -> 0.01 us
  local copies, waits for them, and re-layouts: 36.2 us -> 65 us
  between operations: 14.3 us -> 0.79 us
  blocking collectives: 13.5 us -> 0 us
  matrix products: 40.1 us -> 27.4 us
  other arithmetic: 10.9 us -> 18 us
  starting transfers between devices: 4.51 us -> 7.28 us
    pallas_call x0 -> x1, Pallas kernels: none -> 83.1 us  [fetch(): pl.pallas_call(functools.partial(fetch_kernel, sizes), out_shape=(jax.Sha...]
    all_to_all x1, waiting for transfers between devices: 57.7 us -> 0.01 us  [on_device(): lax.all_to_all(request.reshape(owner_count, pos_capacity), 'item', split_...]
    reshape x6 -> x9, local copies, waits for them, and re-layouts: 17.7 us -> 37.6 us  [the longest x6 24.5 us: by_core(): split = right.reshape(right.shape[0], nx, CORES, -1)]
    all_to_all x1 -> x0, blocking collectives: 13.5 us -> none  [on_device(): lax.all_to_all(request.reshape(owner_count, pos_capacity), 'item', split_...]
    all_gather x1 -> x0, waiting for transfers between devices: 10.2 us -> none  [on_device(): neg_held = lax.all_gather(neg_own, 'item', axis=0, tiled=True)]
    unnamed x28 -> x30, local copies, waits for them, and re-layouts: 0.73 us -> 9.78 us
    dot_general x3 -> x1, matrix products: 14.6 us -> 6.14 us  [tower_grads(): lax.dot_general(out_grad, w_item_out, (((1,), (1,)), ((), ())), preferred...]
    dot_general x2, matrix products: 10.3 us -> 5.73 us  [pick(): jnp.dot(onehot, rows, preferred_element_type=jnp.float32)]
  transfers between devices with their start and end apart: 2 -> 1, of which waited for: 2 -> 0; matrix products, arithmetic and copies ran while one was open for 6% -> 4% of each run, Pallas kernels for 0% -> 0%
where the time goes in v2:
time: 244 us; the launch traced here: 242 us
  Pallas kernels  124 us (51%)
  local copies, waits for them, and re-layouts  65 us (27%)
  matrix products  27.4 us (11%)
  other arithmetic  18 us (7%)
  starting transfers between devices  7.28 us (3%)
    pallas_call x1, Pallas kernels, fetch(): pl.pallas_call(functools.partial(fetch_kernel, sizes), out_shape=(jax.Sha...  83.1 us
    pallas_call x1, Pallas kernels, reduce_grads(): pl.pallas_call(functools.partial(reduce_kernel, sizes), out_shape=jax.Sha...  40.5 us
    reshape x6, local copies, waits for them, and re-layouts, by_core(): split = right.reshape(right.shape[0], nx, CORES, -1)  24.5 us
    reshape x3, local copies, waits for them, and re-layouts, by_core(): return split.transpose(2, 0, 1, 3).reshape(CORES, right.shape[0], -1)  13.1 us
    unnamed x30, local copies, waits for them, and re-layouts  9.78 us
    gather x1, local copies, waits for them, and re-layouts, on_device(): pos_own = jnp.take(item_table, asked.reshape(-1), axis=0, mode='clip')  7.3 us
    all_to_all x1, starting transfers between devices, on_device(): lax.all_to_all(request.reshape(owner_count, pos_capacity), 'item', split_...  7.28 us
    dot_general x1, matrix products, item_tower(): jnp.dot(features, w_item_in, preferred_element_type=jnp.float32)  6.27 us
  transfers between devices with their start and end apart: 1, of which 0 were waited for; matrix products, arithmetic and copies ran while one was open for 4% of the time, Pallas kernels for 0%

profile of v2, /device:TPU:0, one launch (start us, length us, event | category | flops | bytes accessed | tf_op | source)
XLA Modules:
  0.0 242.2 jit_solution(11169664916236615618)
XLA Ops:
  3.9 7.3 %all-to-all-start = ((s32[8,1,96]{2,1,0:T(1,128)}), s32[8,1,96]{2,1,0:T(1,128)S(1)}, u32[]{:S(2)}, u32[]{:S(2)}) async-start(s32[8,1,96]{2,1,0:T(1,128)} %all_to_all.6), calls=%async_computation | async-start | bytes 8192 | tf_op jit(solution)/shard_map/all_to_all | solution.py:393
  12.3 2.1 multiply_reduce_fusion.3
  16.3 4.3 %gather_fusion = bf16[256,1024]{1,0:T(8,128)(2,1)S(1)} fusion(bf16[2048,1024]{1,0:T(8,128)(2,1)} %param.11, s32[1024]{0:T(1024)S(1)} %pad_clamp_fusion.1), kind=kCustom, calls=%fused_computation | custom fusion | bytes 1049600 | tf_op jit(solution)/shard_map/jit(_take)/gather | solution.py:400
  21.8 7.3 %gather_fusion.1 = bf16[768,1024]{1,0:T(8,128)(2,1)} fusion(bf16[2048,1024]{1,0:T(8,128)(2,1)} %param.11, s32[1024]{0:T(1024)S(1)} %pad_clamp_fusion), kind=kCustom, calls=%fused_computation.1 | custom fusion | bytes 3148800 | tf_op jit(solution)/shard_map/jit(_take)/gather | solution.py:401
  30.6 83.1 %shard_map.121 = (bf16[8,256,1024]{2,1,0:T(8,128)(2,1)S(1)}, bf16[8,96,1024]{2,1,0:T(8,128)(2,1)S(1)}) custom-call(bf16[256,1024]{1,0:T(8,128)(2,1)S(1)} %gather_fusion, bf16[8,96,1024]{2,1,0:T(8,128)(2,1)S(1)} %bitcast.27), custom_call_target="tpu_custom_call" | custom-call | flops 1000000 | bytes 100000000 | tf_op jit(solution)/shard_map/pallas_call | solution.py:306
  114.5 4.9 %fusion.3 = bf16[1024,1024]{1,0:T(8,128)(2,1)S(1)} fusion(bf16[2048,1024]{1,0:T(8,128)(2,1)S(1)} %bitcast.30, s32[1024]{0:T(1024)S(1)} %get-tuple-element.10), kind=kOutput, calls=%fused_computation.18 | convolution fusion | flops 4298113024 | bytes 6295552 | tf_op jit(solution)/shard_map/dot_general | solution.py:339
  119.4 1.9 pad_maximum_fusion.features
  121.4 6.3 %multiply_convert_fusion.1 = (bf16[1408,1024]{1,0:T(8,128)(2,1)S(1)}, f32[1408,1024]{1,0:T(8,128)}) fusion(bf16[1024,1024]{1,0:T(8,128)(2,1)S(1)} %copy-done, bf16[384,1024]{1,0:T(8,128)(2,1)S(1)} %convolution_convert_fusion, bf16[1024,1024]{1,0:T(8,128)(2,1)S(1)} %fusion.3), kind=kOutput, calls=%fused_computation.5 | convolution fusion | flops 2965766144 | bytes 13631488 | tf_op jit(solution)/shard_map/dot_general | solution.py:348
  127.6 3.5 %multiply_reduce_fusion.1 = (f32[1408]{0:T(1024)S(1)}, f32[1408,512]{0,1:T(8,128)}) fusion(bf16[1408,1024]{1,0:T(8,128)(2,1)S(1)} %get-tuple-element.15.hidden, bf16[1024,512]{1,0:T(8,128)(2,1)S(1)} %copy-done.13), kind=kOutput, calls=%fused_computation.16 | convolution fusion | flops 1477835392 | bytes 6821376 | tf_op jit(solution)/shard_map/dot_general | solution.py:350
  131.1 3.5 %copy.23 = f32[1408,512]{1,0:T(8,128)} copy(f32[1408,512]{0,1:T(8,128)} %get-tuple-element.18) | data formatting | bytes 5767168 | tf_op jit(solution)/shard_map/dot_general | solution.py:350
  134.6 2.1 multiply_convert_fusion.3
  137.7 2.2 convolution_multiply_fusion
  140.8 2.1 multiply_convert_fusion.4
  145.0 2.0 reshape.95.query_side
  147.0 3.2 %multiply_reduce_fusion = f32[1408]{0:T(1024)S(1)} fusion(f32[1408,512]{1,0:T(8,128)} %copy.23, f32[384,512]{1,0:T(8,128)S(1)} %fusion.7, f32[1024,512]{1,0:T(8,128)} %convolution_multiply_fusion, f32[1408]{0:T(1024)S(1)} %add_rsqrt_fusion), kind=kLoop, calls=%fused_computation.15 | loop fusion | flops 2882176 | bytes 5778432 | tf_op jit(solution)/shard_map/reduce_sum | solution.py:358
  150.9 2.1 multiply_convert_fusion.2
  153.0 4.4 %reshape.98 = bf16[1408,2,2,128]{3,2,1,0:T(2,128)(2,1)} reshape(bf16[1408,512]{1,0:T(8,128)(2,1)} %multiply_convert_fusion.2) | data formatting | bytes 2883584 | tf_op jit(solution)/shard_map/reshape | solution.py:448
  157.5 6.1 %multiply_convert_fusion = bf16[1408,1024]{1,0:T(8,128)(2,1)} fusion(f32[1408,1024]{1,0:T(8,128)} %get-tuple-element.16, bf16[1408,512]{1,0:T(8,128)(2,1)S(1)} %copy-done.10, bf16[1024,512]{1,0:T(8,128)(2,1)} %param.14), kind=kOutput, calls=%fused_computation.4 | convolution fusion | flops 1489371136 | bytes 11141120 | tf_op jit(solution)/shard_map/dot_general | solution.py:360
  163.6 3.4 %copy.35 = bf16[1408,2,2,128]{3,1,0,2:T(2,128)(2,1)} copy(bf16[1408,2,2,128]{3,2,1,0:T(2,128)(2,1)S(1)} %copy-done.11) | data formatting | bytes 2883584 | tf_op jit(solution)/shard_map/reshape | solution.py:448
  167.0 3.6 %reshape.99.out_side = bf16[2,1408,256]{2,1,0:T(8,128)(2,1)S(1)} reshape(bf16[2,1408,2,128]{3,2,1,0:T(2,128)(2,1)} %bitcast.33) | data formatting | bytes 2883584 | tf_op jit(solution)/shard_map/reshape | solution.py:449
  170.7 7.9 %reshape.96 = bf16[1408,2,2,256]{3,2,1,0:T(2,128)(2,1)} reshape(bf16[1408,1024]{1,0:T(8,128)(2,1)} %multiply_convert_fusion) | data formatting | bytes 5767168 | tf_op jit(solution)/shard_map/reshape | solution.py:448
  178.6 6.7 %copy.34 = bf16[1408,2,2,256]{3,1,0,2:T(2,128)(2,1)} copy(bf16[1408,2,2,256]{3,2,1,0:T(2,128)(2,1)} %reshape.96) | data formatting | bytes 5767168 | tf_op jit(solution)/shard_map/reshape | solution.py:448
  185.3 7.4 %reshape.97.in_side = bf16[2,1408,512]{2,1,0:T(8,128)(2,1)} reshape(bf16[2,1408,2,256]{3,2,1,0:T(2,128)(2,1)} %bitcast.32) | data formatting | bytes 5767168 | tf_op jit(solution)/shard_map/reshape | solution.py:449
  200.3 40.5 %shard_map.122 = f32[2,64,512]{2,1,0:T(8,128)S(1)} custom-call(bf16[384,1024]{1,0:T(8,128)(2,1)S(1)} %copy-done.5, bf16[1408,1024]{1,0:T(8,128)(2,1)S(1)} %copy-done.2, bf16[1408,1024]{1,0:T(8,128)(2,1)S(1)} %copy-done.7, bf16[2,384,256]{2,1,0:T(8,128)(2,1)S(1)} %copy-done.4, bf16[2,1408,512]{2,1,0:T(8,128)(2,1)S(1)} %copy-done.3, ...), custom_call_target="tpu_custom_call" | custom-call | flops 10000000000 | bytes 10000000 | tf_op jit(solution)/shard_map/pallas_call | solution.py:176
  (56 shorter events, 23.4 us)
Async XLA Ops:
  0.6 120.7 %copy-start = (bf16[1024,1024]{1,0:T(8,128)(2,1)S(1)}, bf16[1024,1024]{1,0:T(8,128)(2,1)}, u32[]{:S(2)}) copy-start(bf16[1024,1024]{1,0:T(8,128)(2,1)} %param.13) | copy-start | bytes 6291460
  3.9 16.7 %all-to-all-start = ((s32[8,1,96]{2,1,0:T(1,128)}), s32[8,1,96]{2,1,0:T(1,128)S(1)}, u32[]{:S(2)}, u32[]{:S(2)}) async-start(s32[8,1,96]{2,1,0:T(1,128)} %all_to_all.6), calls=%async_computation | async-start | bytes 8192 | tf_op jit(solution)/shard_map/all_to_all | solution.py:393
  14.5 125.4 %copy-start.12 = (f32[384,512]{1,0:T(8,128)}, f32[384,512]{1,0:T(8,128)S(1)}, u32[]{:S(2)}) copy-start(f32[384,512]{1,0:T(8,128)S(1)} %get-tuple-element.20) | copy-start | bytes 2359300
  29.1 1.4 copy-start.1
  121.4 6.3 %copy-start.13 = (bf16[1024,512]{1,0:T(8,128)(2,1)S(1)}, bf16[1024,512]{1,0:T(8,128)(2,1)}, u32[]{:S(2)}) copy-start(bf16[1024,512]{1,0:T(8,128)(2,1)} %param.14) | copy-start | bytes 3145732
  127.6 3.5 %copy-start.6 = (bf16[1408,1024]{1,0:T(8,128)(2,1)}, bf16[1408,1024]{1,0:T(8,128)(2,1)S(1)}, u32[]{:S(2)}) copy-start(bf16[1408,1024]{1,0:T(8,128)(2,1)S(1)} %get-tuple-element.15.hidden) | copy-start | bytes 8650756
  134.6 2.4 copy-start.14
  147.0 3.3 %copy-start.8 = (f32[1408,512]{1,0:T(8,128)S(1)}, f32[1408,512]{1,0:T(8,128)}, u32[]{:S(2)}) copy-start(f32[1408,512]{1,0:T(8,128)} %copy.23) | copy-start | bytes 8650756
  147.0 4.0 %copy-start.9 = (f32[1024,512]{1,0:T(8,128)S(1)}, f32[1024,512]{1,0:T(8,128)}, u32[]{:S(2)}) copy-start(f32[1024,512]{1,0:T(8,128)} %convolution_multiply_fusion) | copy-start | bytes 6291460
  153.0 4.4 %copy-start.10 = (bf16[1408,512]{1,0:T(8,128)(2,1)S(1)}, bf16[1408,512]{1,0:T(8,128)(2,1)}, u32[]{:S(2)}) copy-start(bf16[1408,512]{1,0:T(8,128)(2,1)} %multiply_convert_fusion.2) | copy-start | bytes 4325380
  157.5 6.1 %copy-start.11 = (bf16[1408,2,2,128]{3,2,1,0:T(2,128)(2,1)S(1)}, bf16[1408,2,2,128]{3,2,1,0:T(2,128)(2,1)}, u32[]{:S(2)}) copy-start(bf16[1408,2,2,128]{3,2,1,0:T(2,128)(2,1)} %reshape.98) | copy-start | bytes 4325380
  192.8 1.8 copy-start.2
  194.6 1.8 copy-start.3
  196.4 1.0 copy-start.4
  197.4 1.1 copy-start.5
  198.5 1.8 copy-start.7

commit v3 on v2

--- a/solution.py
+++ b/solution.py
@@ -85,6 +85,18 @@
     span = rows * PARTS
     items = TILE // span
 
+    def side(right, core):
+        if len(right.shape) == 3:
+            return right[core]
+        width = right.shape[1] // (nx * CORES)
+        return jnp.concatenate(
+            [
+                right[:, pl.ds(pl.multiple_of((x * CORES + core) * width, width), width)]
+                for x in range(nx)
+            ],
+            axis=1,
+        )
+
     def products(core):
         def body(tile, carry):
             here = pl.ds(pl.multiple_of(tile * TILE, TILE), TILE)
@@ -93,7 +105,7 @@
                 made.append(
                     lax.dot_general(
                         left[:, here],
-                        right[core],
+                        side(right, core),
                         (((0,), (0,)), ((), ())),
                         preferred_element_type=jnp.float32,
                     ).astype(jnp.bfloat16)
@@ -260,10 +272,9 @@
         copy(pos_own.at[peer], pos_out.at[item], p_send.at[d], p_recv.at[d], peer)
         for d, peer in enumerate(peers)
     ]
-    for made in straight:
-        made.start()
     neg_out[item] = neg_own[...]
     pos_out[item] = pos_own[item]
+    portion = -(-len(straight) // max(1, nz - 1))
     for step in range(1, nz):
         for way in range(2):
             block, there = block_at(way, step)
@@ -276,6 +287,11 @@
                     along_y(way, step, d, block).start()
 
             pl.when(there)(arrived)
+        for made in straight[(step - 1) * portion : step * portion]:
+            made.start()
+    if nz == 1:
+        for made in straight:
+            made.start()
     for made in straight:
         made.wait_recv()
     for d in range(1, ny):
@@ -445,6 +461,8 @@
     in_grad, out_grad = tower_grads(hidden_pre, inverse, unit, upstream, w_item_out)
 
     def by_core(right):
+        if right.shape[1] // query_axis % 128 == 0:
+            return right
         split = right.reshape(right.shape[0], nx, CORES, -1)
         return split.transpose(2, 0, 1, 3).reshape(CORES, right.shape[0], -1)
 

time: 244 us -> 191 us (0.78)
  local copies, waits for them, and re-layouts: 65 us -> 20.9 us
  other arithmetic: 18 us -> 12.6 us
  matrix products: 27.4 us -> 23.2 us
    reshape x9 -> x0, local copies, waits for them, and re-layouts: 37.6 us -> none  [the longest x6 24.5 us: by_core(): split = right.reshape(right.shape[0], nx, CORES, -1)]
    unnamed x30 -> x24, local copies, waits for them, and re-layouts: 9.78 us -> 3.33 us
    dot_general x1, matrix products: 6.14 us -> 3.17 us  [tower_grads(): lax.dot_general(out_grad, w_item_out, (((1,), (1,)), ((), ())), preferred...]
    reduce_sum x1, other arithmetic: 3.18 us -> 0.62 us  [tower_grads(): jnp.sum(unit * upstream, axis=-1, keepdims=True)]
  transfers between devices with their start and end apart: 1 -> 1, of which waited for: 0 -> 0; matrix products, arithmetic and copies ran while one was open for 4% -> 5% of each run, Pallas kernels for 0% -> 0%
where the time goes in v3:
time: 191 us; the launch traced here: 190 us
  Pallas kernels  125 us (65%)
  matrix products  23.2 us (12%)
  local copies, waits for them, and re-layouts  20.9 us (11%)
  other arithmetic  12.6 us (7%)
  starting transfers between devices  7.28 us (4%)
    pallas_call x1, Pallas kernels, fetch(): pl.pallas_call(functools.partial(fetch_kernel, sizes), out_shape=(jax.Sha...  84.9 us
    pallas_call x1, Pallas kernels, reduce_grads(): pl.pallas_call(functools.partial(reduce_kernel, sizes), out_shape=jax.Sha...  40.1 us
    gather x1, local copies, waits for them, and re-layouts, on_device(): pos_own = jnp.take(item_table, asked.reshape(-1), axis=0, mode='clip')  7.3 us
    all_to_all x1, starting transfers between devices, on_device(): lax.all_to_all(request.reshape(owner_count, pos_capacity), 'item', split_...  7.28 us
    dot_general x1, matrix products, item_tower(): jnp.dot(features, w_item_in, preferred_element_type=jnp.float32)  6.3 us
    dot_general x2, matrix products, pick(): jnp.dot(onehot, rows, preferred_element_type=jnp.float32)  5.72 us
    gather x1, local copies, waits for them, and re-layouts, on_device(): neg_own = jnp.take(item_table, own_rows, axis=0, mode='clip')  4.29 us
  transfers between devices with their start and end apart: 1, of which 0 were waited for; matrix products, arithmetic and copies ran while one was open for 5% of the time, Pallas kernels for 0%

profile of v3, /device:TPU:0, one launch (start us, length us, event | category | flops | bytes accessed | tf_op | source)
XLA Modules:
  0.0 190.0 jit_solution(5234728918643583546)
XLA Ops:
  0.6 0.8 reduce
  2.3 0.9 select_reduce_fusion
  3.9 7.3 %all-to-all-start = ((s32[8,1,96]{2,1,0:T(1,128)}), s32[8,1,96]{2,1,0:T(1,128)S(1)}, u32[]{:S(2)}, u32[]{:S(2)}) async-start(s32[8,1,96]{2,1,0:T(1,128)} %all_to_all.6), calls=%async_computation | async-start | bytes 8192 | tf_op jit(solution)/shard_map/all_to_all | solution.py:409
  11.2 1.2 convert_reduce_fusion
  12.3 2.1 %multiply_reduce_fusion.3 = (f32[384]{0:T(512)S(1)}, f32[384,512]{1,0:T(8,128)S(1)}) fusion(bf16[384,1024]{1,0:T(8,128)(2,1)} %queries.1, bf16[1024,512]{1,0:T(8,128)(2,1)} %param.12), kind=kOutput, calls=%fused_computation.37 | convolution fusion | flops 403046016 | bytes 2622976 | tf_op jit(solution)/shard_map/dot_general | solution.py:425
  15.2 1.0 select_reduce_fusion.1
  16.2 4.3 %gather_fusion = bf16[256,1024]{1,0:T(8,128)(2,1)S(1)} fusion(bf16[2048,1024]{1,0:T(8,128)(2,1)} %param.11, s32[1024]{0:T(1024)S(1)} %pad_clamp_fusion.1), kind=kCustom, calls=%fused_computation | custom fusion | bytes 1049600 | tf_op jit(solution)/shard_map/jit(_take)/gather | solution.py:416
  21.8 7.3 %gather_fusion.1 = bf16[768,1024]{1,0:T(8,128)(2,1)} fusion(bf16[2048,1024]{1,0:T(8,128)(2,1)} %param.11, s32[1024]{0:T(1024)S(1)} %pad_clamp_fusion), kind=kCustom, calls=%fused_computation.1 | custom fusion | bytes 3148800 | tf_op jit(solution)/shard_map/jit(_take)/gather | solution.py:417
  29.1 1.4 copy-done.1
  30.5 84.9 %shard_map.121 = (bf16[8,256,1024]{2,1,0:T(8,128)(2,1)S(1)}, bf16[8,96,1024]{2,1,0:T(8,128)(2,1)S(1)}) custom-call(bf16[256,1024]{1,0:T(8,128)(2,1)S(1)} %gather_fusion, bf16[8,96,1024]{2,1,0:T(8,128)(2,1)S(1)} %bitcast.18), custom_call_target="tpu_custom_call" | custom-call | flops 1000000 | bytes 100000000 | tf_op jit(solution)/shard_map/pallas_call | solution.py:322
  115.4 0.8 convolution_convert_fusion
  116.2 4.9 %fusion.3 = bf16[1024,1024]{1,0:T(8,128)(2,1)S(1)} fusion(bf16[2048,1024]{1,0:T(8,128)(2,1)S(1)} %bitcast.21, s32[1024]{0:T(1024)S(1)} %get-tuple-element.10), kind=kOutput, calls=%fused_computation.17 | convolution fusion | flops 4298113024 | bytes 6295552 | tf_op jit(solution)/shard_map/dot_general | solution.py:355
  121.2 1.8 pad_maximum_fusion.features
  123.0 6.3 %multiply_convert_fusion.1 = (bf16[1408,1024]{1,0:T(8,128)(2,1)S(1)}, f32[1408,1024]{1,0:T(8,128)}) fusion(bf16[1024,1024]{1,0:T(8,128)(2,1)S(1)} %copy-done, bf16[384,1024]{1,0:T(8,128)(2,1)S(1)} %convolution_convert_fusion, bf16[1024,1024]{1,0:T(8,128)(2,1)S(1)} %fusion.3), kind=kOutput, calls=%fused_computation.5 | convolution fusion | flops 2965766144 | bytes 13631488 | tf_op jit(solution)/shard_map/dot_general | solution.py:364
  129.3 3.6 %multiply_reduce_fusion.1 = (f32[1408]{0:T(1024)S(1)}, f32[1408,512]{0,1:T(8,128)}) fusion(bf16[1408,1024]{1,0:T(8,128)(2,1)S(1)} %get-tuple-element.15.hidden, bf16[1024,512]{1,0:T(8,128)(2,1)S(1)} %copy-done.7), kind=kOutput, calls=%fused_computation.15 | convolution fusion | flops 1477835392 | bytes 6821376 | tf_op jit(solution)/shard_map/dot_general | solution.py:366
  132.9 3.4 %copy.14 = f32[1408,512]{1,0:T(8,128)} copy(f32[1408,512]{0,1:T(8,128)} %get-tuple-element.18) | data formatting | bytes 5767168 | tf_op jit(solution)/shard_map/dot_general | solution.py:366
  136.3 2.1 %multiply_convert_fusion.3 = bf16[1408,512]{1,0:T(8,128)(2,1)S(1)} fusion(f32[1408,512]{1,0:T(8,128)} %copy.14, f32[1408]{0:T(1024)S(1)} %add_rsqrt_fusion), kind=kLoop, calls=%fused_computation.16 | loop fusion | flops 1441792 | bytes 4331008 | tf_op jit(solution)/shard_map/convert_element_type | solution.py:369
  138.7 0.7 fusion.14
  139.4 0.9 convolution_multiply_fusion
  140.3 0.8 multiply_reduce_fusion.2
  141.3 0.9 copy-done.6
  142.8 1.3 multiply_convert_fusion.2.out_side
  145.3 3.2 %multiply_convert_fusion.in_side = bf16[1408,1024]{1,0:T(8,128)(2,1)S(1)} fusion(f32[1408,1024]{1,0:T(8,128)S(1)} %bitcast.28, bf16[1408,512]{1,0:T(8,128)(2,1)S(1)} %multiply_convert_fusion.2.out_side, bf16[1024,512]{1,0:T(8,128)(2,1)S(1)} %copy-done.8), kind=kOutput, calls=%fused_computation.4 | convolution fusion | flops 1489371136 | bytes 11141120 | tf_op jit(solution)/shard_map/dot_general | solution.py:376
  148.5 40.1 %shard_map.122 = f32[2,64,512]{2,1,0:T(8,128)S(1)} custom-call(bf16[384,1024]{1,0:T(8,128)(2,1)S(1)} %copy-done.3, bf16[1408,1024]{1,0:T(8,128)(2,1)S(1)} %copy-done.2, bf16[1408,1024]{1,0:T(8,128)(2,1)S(1)} %copy-done.5, bf16[384,512]{1,0:T(8,128)(2,1)S(1)} %multiply_convert_fusion.4.query_side, bf16[1408,1024]{1,0:T(8,128)(2,1)S(1)} %multiply_convert_fusion.in_side, ...), custom_call_target="tpu_custom_call" | custom-call | flops 10000000000 | bytes 10000000 | tf_op jit(solution)/shard_map/pallas_call | solution.py:188
  (42 shorter events, 7.1 us)
Async XLA Ops:
  0.6 122.4 %copy-start = (bf16[1024,1024]{1,0:T(8,128)(2,1)S(1)}, bf16[1024,1024]{1,0:T(8,128)(2,1)}, u32[]{:S(2)}) copy-start(bf16[1024,1024]{1,0:T(8,128)(2,1)} %param.13) | copy-start | bytes 6291460
  3.9 16.6 %all-to-all-start = ((s32[8,1,96]{2,1,0:T(1,128)}), s32[8,1,96]{2,1,0:T(1,128)S(1)}, u32[]{:S(2)}, u32[]{:S(2)}) async-start(s32[8,1,96]{2,1,0:T(1,128)} %all_to_all.6), calls=%async_computation | async-start | bytes 8192 | tf_op jit(solution)/shard_map/all_to_all | solution.py:409
  29.1 1.4 copy-start.1
  123.0 6.3 %copy-start.7 = (bf16[1024,512]{1,0:T(8,128)(2,1)S(1)}, bf16[1024,512]{1,0:T(8,128)(2,1)}, u32[]{:S(2)}) copy-start(bf16[1024,512]{1,0:T(8,128)(2,1)} %param.14) | copy-start | bytes 3145732
  129.3 3.6 %copy-start.4 = (bf16[1408,1024]{1,0:T(8,128)(2,1)}, bf16[1408,1024]{1,0:T(8,128)(2,1)S(1)}, u32[]{:S(2)}) copy-start(bf16[1408,1024]{1,0:T(8,128)(2,1)S(1)} %get-tuple-element.15.hidden) | copy-start | bytes 8650756
  136.3 2.4 %copy-start.9 = (f32[1,1024]{1,0:T(1,128)S(1)}, f32[1,1024]{1,0:T(1,128)}, u32[]{:S(2)}) copy-start(f32[1,1024]{1,0:T(1,128)} %param.19) | copy-start | bytes 12292
  140.3 1.8 copy-start.6
  142.1 2.2 %slice-start = ((s8[5767168]{0:T(1024)(128)(4,1)}), s8[4194304]{0:T(1024)(128)(4,1)S(1)}, s32[]{:S(2)}) async-start(s8[5767168]{0:T(1024)(128)(4,1)} %bitcast.27), calls=%async_computation.1 | async-start | bytes 8388608
  142.8 2.0 %copy-start.8 = (bf16[1024,512]{1,0:T(8,128)(2,1)S(1)}, bf16[1024,512]{1,0:T(8,128)(2,1)}, u32[]{:S(2)}) copy-start(bf16[1024,512]{1,0:T(8,128)(2,1)} %param.14) | copy-start | bytes 3145732
  142.8 2.5 %slice-start.1 = ((s8[5767168]{0:T(1024)(128)(4,1)}), s8[1572864]{0:T(1024)(128)(4,1)S(1)}, s32[]{:S(2)}) async-start(s8[5767168]{0:T(1024)(128)(4,1)} %bitcast.27), calls=%async_computation.2 | async-start | bytes 3145728
  145.3 3.2 %copy-start.2 = (bf16[1408,1024]{1,0:T(8,128)(2,1)S(1)}, bf16[1408,1024]{1,0:T(8,128)(2,1)}, u32[]{:S(2)}) copy-start(bf16[1408,1024]{1,0:T(8,128)(2,1)} %pad_maximum_fusion.features) | copy-start | bytes 8650756
  145.3 3.2 %copy-start.3 = (bf16[384,1024]{1,0:T(8,128)(2,1)S(1)}, bf16[384,1024]{1,0:T(8,128)(2,1)}, u32[]{:S(2)}) copy-start(bf16[384,1024]{1,0:T(8,128)(2,1)} %queries.1) | copy-start | bytes 2359300
  145.3 3.2 %copy-start.5 = (bf16[1408,1024]{1,0:T(8,128)(2,1)S(1)}, bf16[1408,1024]{1,0:T(8,128)(2,1)}, u32[]{:S(2)}) copy-start(bf16[1408,1024]{1,0:T(8,128)(2,1)} %copy-done.4) | copy-start | bytes 8650756

commit v4 on v3

--- a/solution.py
+++ b/solution.py
@@ -14,6 +14,7 @@
 PARTS = 2
 DEPTH = 4
 TILE = 256
+HALVES = 2
 
 
 def add_tiles(shape, left, right, out):
@@ -235,24 +236,39 @@
             device_id_type=pl.DeviceIdType.MESH,
         )
 
-    def along_z(way, step, block):
-        source = neg_own if step == 0 else neg_out.at[block * ny + my_y]
+    size = neg_own.shape[0] // HALVES
+
+    def source_of(step, block, half):
+        rows = pl.ds(half * size, size)
+        return neg_own.at[rows] if step == 0 else neg_out.at[block * ny + my_y, rows]
+
+    def along_z(way, step, block, half):
         to = (my_z + (1 if way == 0 else -1) + nz) % nz
         return copy(
-            source, neg_out.at[block * ny + my_y], z_send.at[way, step], z_recv.at[way, step], to * ny + my_y
-        )
-
-    def along_y(way, step, d, block):
-        source = neg_own if step == 0 else neg_out.at[block * ny + my_y]
-        to = my_z * ny + lax.rem(my_y + d, ny)
+            source_of(step, block, half),
+            neg_out.at[block * ny + my_y, pl.ds(half * size, size)],
+            z_send.at[way, step, half],
+            z_recv.at[way, step, half],
+            to * ny + my_y,
+        )
+
+    def along_y(way, step, d, block, half):
         return copy(
-            source, neg_out.at[block * ny + my_y], y_send.at[way, step, d - 1], y_recv.at[way, step, d - 1], to
-        )
-
-    def from_y(way, step, d, block):
+            source_of(step, block, half),
+            neg_out.at[block * ny + my_y, pl.ds(half * size, size)],
+            y_send.at[way, step, d - 1, half],
+            y_recv.at[way, step, d - 1, half],
+            my_z * ny + lax.rem(my_y + d, ny),
+        )
+
+    def from_y(way, step, d, block, half):
         other = lax.rem(my_y + ny - d, ny)
+        rows = pl.ds(half * size, size)
         return copy(
-            neg_own, neg_out.at[block * ny + other], y_send.at[way, step, d - 1], y_recv.at[way, step, d - 1],
+            neg_own.at[rows],
+            neg_out.at[block * ny + other, rows],
+            y_send.at[way, step, d - 1, half],
+            y_recv.at[way, step, d - 1, half],
             my_z * ny + other,
         )
 
@@ -263,54 +279,61 @@
     def has_next(way):
         return my_z < nz - 1 if way == 0 else my_z > 0
 
-    for way in range(2):
-        if nz > 1:
-            pl.when(has_next(way))(lambda way=way: along_z(way, 0, my_z).start())
-    for d in range(1, ny):
-        along_y(0, 0, d, my_z).start()
+    for half in range(HALVES):
+        for way in range(2):
+            if nz > 1:
+                pl.when(has_next(way))(lambda way=way, half=half: along_z(way, 0, my_z, half).start())
+        for d in range(1, ny):
+            along_y(0, 0, d, my_z, half).start()
     straight = [
         copy(pos_own.at[peer], pos_out.at[item], p_send.at[d], p_recv.at[d], peer)
         for d, peer in enumerate(peers)
     ]
     neg_out[item] = neg_own[...]
     pos_out[item] = pos_own[item]
-    portion = -(-len(straight) // max(1, nz - 1))
+    stages = max(1, (nz - 1) * HALVES)
+    bounds = [len(straight) * k // stages for k in range(stages + 1)]
     for step in range(1, nz):
-        for way in range(2):
-            block, there = block_at(way, step)
-
-            def arrived(way=way, step=step, block=block):
-                along_z(way, step - 1, block).wait_recv()
-                if step < nz - 1:
-                    pl.when(has_next(way))(lambda: along_z(way, step, block).start())
-                for d in range(1, ny):
-                    along_y(way, step, d, block).start()
-
-            pl.when(there)(arrived)
-        for made in straight[(step - 1) * portion : step * portion]:
-            made.start()
+        for half in range(HALVES):
+            for way in range(2):
+                block, there = block_at(way, step)
+
+                def arrived(way=way, step=step, block=block, half=half):
+                    along_z(way, step - 1, block, half).wait_recv()
+                    if step < nz - 1:
+                        pl.when(has_next(way))(lambda: along_z(way, step, block, half).start())
+                    for d in range(1, ny):
+                        along_y(way, step, d, block, half).start()
+
+                pl.when(there)(arrived)
+            stage = (step - 1) * HALVES + half
+            for made in straight[bounds[stage] : bounds[stage + 1]]:
+                made.start()
     if nz == 1:
         for made in straight:
             made.start()
     for made in straight:
         made.wait_recv()
-    for d in range(1, ny):
-        from_y(0, 0, d, my_z).wait_recv()
-        along_y(0, 0, d, my_z).wait_send()
-    for way in range(2):
-        if nz > 1:
-            pl.when(has_next(way))(lambda way=way: along_z(way, 0, my_z).wait_send())
-        for step in range(1, nz):
-            block, there = block_at(way, step)
-
-            def finished(way=way, step=step, block=block):
-                if step < nz - 1:
-                    pl.when(has_next(way))(lambda: along_z(way, step, block).wait_send())
-                for d in range(1, ny):
-                    from_y(way, step, d, block).wait_recv()
-                    along_y(way, step, d, block).wait_send()
-
-            pl.when(there)(finished)
+    for half in range(HALVES):
+        for d in range(1, ny):
+            from_y(0, 0, d, my_z, half).wait_recv()
+            along_y(0, 0, d, my_z, half).wait_send()
+        for way in range(2):
+            if nz > 1:
+                pl.when(has_next(way))(
+                    lambda way=way, half=half: along_z(way, 0, my_z, half).wait_send()
+                )
+            for step in range(1, nz):
+                block, there = block_at(way, step)
+
+                def finished(way=way, step=step, block=block, half=half):
+                    if step < nz - 1:
+                        pl.when(has_next(way))(lambda: along_z(way, step, block, half).wait_send())
+                    for d in range(1, ny):
+                        from_y(way, step, d, block, half).wait_recv()
+                        along_y(way, step, d, block, half).wait_send()
+
+                pl.when(there)(finished)
     for made in straight:
         made.wait_send()
 
@@ -328,10 +351,10 @@
         in_specs=[pl.BlockSpec(memory_space=pltpu.VMEM)] * 2,
         out_specs=(pl.BlockSpec(memory_space=pltpu.VMEM),) * 2,
         scratch_shapes=[
-            pltpu.SemaphoreType.DMA((2, steps)),
-            pltpu.SemaphoreType.DMA((2, steps)),
-            pltpu.SemaphoreType.DMA((2, steps, fans)),
-            pltpu.SemaphoreType.DMA((2, steps, fans)),
+            pltpu.SemaphoreType.DMA((2, steps, HALVES)),
+            pltpu.SemaphoreType.DMA((2, steps, HALVES)),
+            pltpu.SemaphoreType.DMA((2, steps, fans, HALVES)),
+            pltpu.SemaphoreType.DMA((2, steps, fans, HALVES)),
             pltpu.SemaphoreType.DMA((item_count - 1,)),
             pltpu.SemaphoreType.DMA((item_count - 1,)),
         ],

time: 191 us -> 180 us (0.942)
  Pallas kernels: 125 us -> 114 us
    pallas_call x1, Pallas kernels: 84.9 us -> 75.4 us  [fetch(): pl.pallas_call(functools.partial(fetch_kernel, sizes), out_shape=(jax.Sha...]
where the time goes in v4:
time: 180 us; the launch traced here: 179 us
  Pallas kernels  114 us (63%)
  matrix products  23.2 us (13%)
  local copies, waits for them, and re-layouts  20.9 us (12%)
  other arithmetic  12.6 us (7%)
  starting transfers between devices  7.28 us (4%)
    pallas_call x1, Pallas kernels, fetch(): pl.pallas_call(functools.partial(fetch_kernel, sizes), out_shape=(jax.Sha...  75.4 us
    pallas_call x1, Pallas kernels, reduce_grads(): pl.pallas_call(functools.partial(reduce_kernel, sizes), out_shape=jax.Sha...  38.7 us
    gather x1, local copies, waits for them, and re-layouts, on_device(): pos_own = jnp.take(item_table, asked.reshape(-1), axis=0, mode='clip')  7.3 us
    all_to_all x1, starting transfers between devices, on_device(): lax.all_to_all(request.reshape(owner_count, pos_capacity), 'item', split_...  7.28 us
    dot_general x1, matrix products, item_tower(): jnp.dot(features, w_item_in, preferred_element_type=jnp.float32)  6.29 us
    dot_general x2, matrix products, pick(): jnp.dot(onehot, rows, preferred_element_type=jnp.float32)  5.73 us
    gather x1, local copies, waits for them, and re-layouts, on_device(): neg_own = jnp.take(item_table, own_rows, axis=0, mode='clip')  4.29 us
  transfers between devices with their start and end apart: 1, of which 0 were waited for; matrix products, arithmetic and copies ran while one was open for 5% of the time, Pallas kernels for 0%

profile of v4, /device:TPU:0, one launch (start us, length us, event | category | flops | bytes accessed | tf_op | source)
XLA Modules:
  0.0 179.0 jit_solution(3022012129584778198)
XLA Ops:
  0.6 0.8 reduce
  2.3 0.9 select_reduce_fusion
  3.9 7.3 %all-to-all-start = ((s32[8,1,96]{2,1,0:T(1,128)}), s32[8,1,96]{2,1,0:T(1,128)S(1)}, u32[]{:S(2)}, u32[]{:S(2)}) async-start(s32[8,1,96]{2,1,0:T(1,128)} %all_to_all.6), calls=%async_computation | async-start | bytes 8192 | tf_op jit(solution)/shard_map/all_to_all | solution.py:432
  11.2 1.2 convert_reduce_fusion
  12.3 2.1 %multiply_reduce_fusion.3 = (f32[384]{0:T(512)S(1)}, f32[384,512]{1,0:T(8,128)S(1)}) fusion(bf16[384,1024]{1,0:T(8,128)(2,1)} %queries.1, bf16[1024,512]{1,0:T(8,128)(2,1)} %param.12), kind=kOutput, calls=%fused_computation.37 | convolution fusion | flops 403046016 | bytes 2622976 | tf_op jit(solution)/shard_map/dot_general | solution.py:448
  15.2 1.0 select_reduce_fusion.1
  16.2 4.3 %gather_fusion = bf16[256,1024]{1,0:T(8,128)(2,1)S(1)} fusion(bf16[2048,1024]{1,0:T(8,128)(2,1)} %param.11, s32[1024]{0:T(1024)S(1)} %pad_clamp_fusion.1), kind=kCustom, calls=%fused_computation | custom fusion | bytes 1049600 | tf_op jit(solution)/shard_map/jit(_take)/gather | solution.py:439
  21.8 7.3 %gather_fusion.1 = bf16[768,1024]{1,0:T(8,128)(2,1)} fusion(bf16[2048,1024]{1,0:T(8,128)(2,1)} %param.11, s32[1024]{0:T(1024)S(1)} %pad_clamp_fusion), kind=kCustom, calls=%fused_computation.1 | custom fusion | bytes 3148800 | tf_op jit(solution)/shard_map/jit(_take)/gather | solution.py:440
  29.1 1.4 copy-done.1
  30.5 75.4 %shard_map.121 = (bf16[8,256,1024]{2,1,0:T(8,128)(2,1)S(1)}, bf16[8,96,1024]{2,1,0:T(8,128)(2,1)S(1)}) custom-call(bf16[256,1024]{1,0:T(8,128)(2,1)S(1)} %gather_fusion, bf16[8,96,1024]{2,1,0:T(8,128)(2,1)S(1)} %bitcast.18), custom_call_target="tpu_custom_call" | custom-call | flops 1000000 | bytes 100000000 | tf_op jit(solution)/shard_map/pallas_call | solution.py:345
  105.9 0.8 convolution_convert_fusion
  106.7 4.9 %fusion.3 = bf16[1024,1024]{1,0:T(8,128)(2,1)S(1)} fusion(bf16[2048,1024]{1,0:T(8,128)(2,1)S(1)} %bitcast.21, s32[1024]{0:T(1024)S(1)} %get-tuple-element.10), kind=kOutput, calls=%fused_computation.17 | convolution fusion | flops 4298113024 | bytes 6295552 | tf_op jit(solution)/shard_map/dot_general | solution.py:378
  111.6 1.8 %pad_maximum_fusion.features = bf16[1408,1024]{1,0:T(8,128)(2,1)} fusion(bf16[384,1024]{1,0:T(8,128)(2,1)S(1)} %convolution_convert_fusion, bf16[1024,1024]{1,0:T(8,128)(2,1)S(1)} %fusion.3), kind=kLoop, calls=%fused_computation.11 | loop fusion | flops 5767168 | bytes 5767168 | tf_op jit(solution)/shard_map/concatenate | solution.py:453
  113.5 6.3 %multiply_convert_fusion.1 = (bf16[1408,1024]{1,0:T(8,128)(2,1)S(1)}, f32[1408,1024]{1,0:T(8,128)}) fusion(bf16[1024,1024]{1,0:T(8,128)(2,1)S(1)} %copy-done, bf16[384,1024]{1,0:T(8,128)(2,1)S(1)} %convolution_convert_fusion, bf16[1024,1024]{1,0:T(8,128)(2,1)S(1)} %fusion.3), kind=kOutput, calls=%fused_computation.5 | convolution fusion | flops 2965766144 | bytes 13631488 | tf_op jit(solution)/shard_map/dot_general | solution.py:387
  119.8 3.6 %multiply_reduce_fusion.1 = (f32[1408]{0:T(1024)S(1)}, f32[1408,512]{0,1:T(8,128)}) fusion(bf16[1408,1024]{1,0:T(8,128)(2,1)S(1)} %get-tuple-element.15.hidden, bf16[1024,512]{1,0:T(8,128)(2,1)S(1)} %copy-done.7), kind=kOutput, calls=%fused_computation.15 | convolution fusion | flops 1477835392 | bytes 6821376 | tf_op jit(solution)/shard_map/dot_general | solution.py:389
  123.3 3.4 %copy.14 = f32[1408,512]{1,0:T(8,128)} copy(f32[1408,512]{0,1:T(8,128)} %get-tuple-element.18) | data formatting | bytes 5767168 | tf_op jit(solution)/shard_map/dot_general | solution.py:389
  126.8 2.1 %multiply_convert_fusion.3 = bf16[1408,512]{1,0:T(8,128)(2,1)S(1)} fusion(f32[1408,512]{1,0:T(8,128)} %copy.14, f32[1408]{0:T(1024)S(1)} %add_rsqrt_fusion), kind=kLoop, calls=%fused_computation.16 | loop fusion | flops 1441792 | bytes 4331008 | tf_op jit(solution)/shard_map/convert_element_type | solution.py:392
  129.2 0.7 fusion.14
  129.9 0.9 convolution_multiply_fusion
  130.8 0.8 multiply_reduce_fusion.2
  131.7 0.9 copy-done.6
  133.2 1.3 multiply_convert_fusion.2.out_side
  135.8 3.2 %multiply_convert_fusion.in_side = bf16[1408,1024]{1,0:T(8,128)(2,1)S(1)} fusion(f32[1408,1024]{1,0:T(8,128)S(1)} %bitcast.28, bf16[1408,512]{1,0:T(8,128)(2,1)S(1)} %multiply_convert_fusion.2.out_side, bf16[1024,512]{1,0:T(8,128)(2,1)S(1)} %copy-done.8), kind=kOutput, calls=%fused_computation.4 | convolution fusion | flops 1489371136 | bytes 11141120 | tf_op jit(solution)/shard_map/dot_general | solution.py:399
  139.0 38.7 %shard_map.122 = f32[2,64,512]{2,1,0:T(8,128)S(1)} custom-call(bf16[384,1024]{1,0:T(8,128)(2,1)S(1)} %copy-done.3, bf16[1408,1024]{1,0:T(8,128)(2,1)S(1)} %copy-done.2, bf16[1408,1024]{1,0:T(8,128)(2,1)S(1)} %copy-done.5, bf16[384,512]{1,0:T(8,128)(2,1)S(1)} %multiply_convert_fusion.4.query_side, bf16[1408,1024]{1,0:T(8,128)(2,1)S(1)} %multiply_convert_fusion.in_side, ...), custom_call_target="tpu_custom_call" | custom-call | flops 10000000000 | bytes 10000000 | tf_op jit(solution)/shard_map/pallas_call | solution.py:189
  (42 shorter events, 7.1 us)
Async XLA Ops:
  0.6 112.8 %copy-start = (bf16[1024,1024]{1,0:T(8,128)(2,1)S(1)}, bf16[1024,1024]{1,0:T(8,128)(2,1)}, u32[]{:S(2)}) copy-start(bf16[1024,1024]{1,0:T(8,128)(2,1)} %param.13) | copy-start | bytes 6291460
  3.9 16.6 %all-to-all-start = ((s32[8,1,96]{2,1,0:T(1,128)}), s32[8,1,96]{2,1,0:T(1,128)S(1)}, u32[]{:S(2)}, u32[]{:S(2)}) async-start(s32[8,1,96]{2,1,0:T(1,128)} %all_to_all.6), calls=%async_computation | async-start | bytes 8192 | tf_op jit(solution)/shard_map/all_to_all | solution.py:432
  29.1 1.4 copy-start.1
  113.5 6.3 %copy-start.7 = (bf16[1024,512]{1,0:T(8,128)(2,1)S(1)}, bf16[1024,512]{1,0:T(8,128)(2,1)}, u32[]{:S(2)}) copy-start(bf16[1024,512]{1,0:T(8,128)(2,1)} %param.14) | copy-start | bytes 3145732
  119.8 3.6 %copy-start.4 = (bf16[1408,1024]{1,0:T(8,128)(2,1)}, bf16[1408,1024]{1,0:T(8,128)(2,1)S(1)}, u32[]{:S(2)}) copy-start(bf16[1408,1024]{1,0:T(8,128)(2,1)S(1)} %get-tuple-element.15.hidden) | copy-start | bytes 8650756
  126.8 2.4 %copy-start.9 = (f32[1,1024]{1,0:T(1,128)S(1)}, f32[1,1024]{1,0:T(1,128)}, u32[]{:S(2)}) copy-start(f32[1,1024]{1,0:T(1,128)} %param.19) | copy-start | bytes 12292
  130.8 1.8 %copy-start.6 = (f32[1408,512]{1,0:T(8,128)S(1)}, f32[1408,512]{1,0:T(8,128)}, u32[]{:S(2)}) copy-start(f32[1408,512]{1,0:T(8,128)} %copy.14) | copy-start | bytes 8650756
  132.6 2.2 %slice-start = ((s8[5767168]{0:T(1024)(128)(4,1)}), s8[4194304]{0:T(1024)(128)(4,1)S(1)}, s32[]{:S(2)}) async-start(s8[5767168]{0:T(1024)(128)(4,1)} %bitcast.27), calls=%async_computation.1 | async-start | bytes 8388608
  133.2 2.0 %copy-start.8 = (bf16[1024,512]{1,0:T(8,128)(2,1)S(1)}, bf16[1024,512]{1,0:T(8,128)(2,1)}, u32[]{:S(2)}) copy-start(bf16[1024,512]{1,0:T(8,128)(2,1)} %param.14) | copy-start | bytes 3145732
  133.2 2.5 %slice-start.1 = ((s8[5767168]{0:T(1024)(128)(4,1)}), s8[1572864]{0:T(1024)(128)(4,1)S(1)}, s32[]{:S(2)}) async-start(s8[5767168]{0:T(1024)(128)(4,1)} %bitcast.27), calls=%async_computation.2 | async-start | bytes 3145728
  135.7 3.2 %copy-start.2 = (bf16[1408,1024]{1,0:T(8,128)(2,1)S(1)}, bf16[1408,1024]{1,0:T(8,128)(2,1)}, u32[]{:S(2)}) copy-start(bf16[1408,1024]{1,0:T(8,128)(2,1)} %pad_maximum_fusion.features) | copy-start | bytes 8650756
  135.7 3.2 %copy-start.3 = (bf16[384,1024]{1,0:T(8,128)(2,1)S(1)}, bf16[384,1024]{1,0:T(8,128)(2,1)}, u32[]{:S(2)}) copy-start(bf16[384,1024]{1,0:T(8,128)(2,1)} %queries.1) | copy-start | bytes 2359300
  135.8 3.2 %copy-start.5 = (bf16[1408,1024]{1,0:T(8,128)(2,1)S(1)}, bf16[1408,1024]{1,0:T(8,128)(2,1)}, u32[]{:S(2)}) copy-start(bf16[1408,1024]{1,0:T(8,128)(2,1)} %copy-done.4) | copy-start | bytes 8650756
